TPU v7x, 32 devices: a whole 2x2x4 slice. The times are simulated.
32 devices in a mesh: cuts: 4 (over z), group: 8 (over y, x, core).
Axes of the slice: x: 2, y: 2, z: 4, core: 2. Of those that a mesh axis runs over, the one named last changes fastest.
Arguments:
- radiation: float32 [32, 2, 128, 128], P(('cuts', 'group')), may hold values from -6 to 6
- phases: float32 [32, 16, 128], P(('cuts', 'group')), may hold values from -3.140625 to 3.140625
- energy: float32 [32, 16, 128], P(('cuts', 'group')), may hold values from -5 to 5
- pixels: int32 [32, 16, 128], P(('cuts', 'group')), may hold values from 0 to 16383
- destination: int32 [32, 16], P(('cuts', 'group')), may hold values from 0 to 3, as said below
- propagator: float32 [2, 128, 128], replicated, may hold values from -1 to 1
- transmit: float32 [2, 32], replicated, may hold values from -1 to 1
Outputs:
- radiation_out: float32 [32, 2, 128, 128], P(('cuts', 'group'))
Inputs may be any that keep to these rules, and one draw needn't show every extreme that they name: `destination`: the blocks of one slice go to exactly 2 different cuts, 8 blocks to each; in every draw some cut receives 8 blocks from every slice of the same position within a cut.
All inputs are finite; a program needn't handle non-finite values.
Results may differ from a plain program's by a relative error of at most 0.0011.
Values sent between devices are 32-bit elements; how exact they have to be, the bound alone decides.
No kernel may reach another device: no remote copies, remote signals or barrier semaphores. Data moves between devices by JAX's collectives and lax.ppermute only.
A program may use at most 64 MiB of HBM per device.

v0:
```python
import math

import jax
import jax.numpy as jnp
from jax import lax
from jax.sharding import PartitionSpec as P

STEPS = 2


KICK_RATE = 0.5
PHASE_RATE = 1.0
EMIT_RATE = 0.5


def from_behind(block, axis, distance):
    devices = range(lax.axis_size(axis))
    route = [(i - distance, i) for i in devices if i - distance in devices]
    return lax.ppermute(block, axis, route)


def matmul(left, right):
    return jnp.dot(left, right, precision=lax.Precision.HIGHEST, preferred_element_type=jnp.float32)


def angle_table(first_ids, second_ids, total_slices):
    product = first_ids[:, None] * second_ids[None, :] % total_slices
    angle = product.astype(jnp.float32) * (2.0 * math.pi / total_slices)
    return (jnp.cos(angle), jnp.sin(angle))


def undulate(field_now, phases, energy, pixels, propagator):
    grid_size = field_now.shape[-1]
    grid_ids = jnp.arange(grid_size, dtype=jnp.int32)
    row_hot = (pixels[:, None] // grid_size == grid_ids[None, :]).astype(jnp.bfloat16)
    col_match = pixels[:, None] % grid_size == grid_ids[None, :]
    col_hot = col_match.astype(jnp.float32)
    field_low = jnp.concatenate([field_now[0], field_now[1]], axis=1).astype(jnp.bfloat16)
    picked = jnp.dot(row_hot, field_low, preferred_element_type=jnp.float32)
    read_real = jnp.sum(picked[:, :grid_size] * col_hot, axis=1)
    read_imag = jnp.sum(picked[:, grid_size:] * col_hot, axis=1)
    energy = energy - KICK_RATE * (read_real * jnp.cos(phases) - read_imag * jnp.sin(phases))
    phases = phases + PHASE_RATE * energy
    weight_real = jnp.cos(phases).astype(jnp.bfloat16)
    weight_imag = (-jnp.sin(phases)).astype(jnp.bfloat16)
    col_low = col_match.astype(jnp.bfloat16)
    spread = jnp.concatenate(
        [col_low * weight_real[:, None], col_low * weight_imag[:, None]], axis=1
    )
    source = lax.dot_general(
        row_hot, spread, (((0,), (0,)), ((), ())), preferred_element_type=jnp.float32
    )
    emitted_real = field_now[0] + EMIT_RATE * source[:, :grid_size]
    emitted_imag = field_now[1] + EMIT_RATE * source[:, grid_size:]
    prop_real = propagator[0]
    prop_imag = propagator[1]
    left_real = matmul(prop_real, emitted_real) - matmul(prop_imag, emitted_imag)
    left_imag = matmul(prop_real, emitted_imag) + matmul(prop_imag, emitted_real)
    out_real = matmul(left_real, prop_real.T) - matmul(left_imag, prop_imag.T)
    out_imag = matmul(left_real, prop_imag.T) + matmul(left_imag, prop_real.T)
    new_field = jnp.stack([out_real, out_imag])
    slipped = from_behind(new_field, ("cuts", "group"), 1)
    return (slipped, phases, energy)


def crystal_filter(field_now, transmit):
    pixel_parts = lax.all_to_all(field_now[None], "group", split_axis=2, concat_axis=0, tiled=True)
    members = pixel_parts.shape[0]
    row_part = pixel_parts.shape[2]
    grid_size = pixel_parts.shape[3]
    pixel_span = row_part * grid_size
    cut_count = lax.axis_size("cuts")
    total_slices = members * cut_count
    data_real = pixel_parts[:, 0].reshape(members, pixel_span)
    data_imag = pixel_parts[:, 1].reshape(members, pixel_span)
    share = -(-pixel_span // cut_count)
    padded_span = share * cut_count
    stacked = jnp.stack([data_real, data_imag], axis=1)
    stacked = jnp.pad(stacked, ((0, 0), (0, 0), (0, padded_span - pixel_span)))
    stacked = stacked.reshape(members, 2, cut_count, share)
    cells = lax.all_to_all(stacked, "cuts", split_axis=2, concat_axis=0, tiled=True)
    cells = cells.reshape(total_slices, 2, share)
    cell_real = cells[:, 0]
    cell_imag = cells[:, 1]
    all_times = jnp.arange(total_slices, dtype=jnp.int32)
    cosine, sine_part = angle_table(all_times, all_times, total_slices)
    spec_real = matmul(cosine, cell_real) + matmul(sine_part, cell_imag)
    spec_imag = matmul(cosine, cell_imag) - matmul(sine_part, cell_real)
    gain_real = transmit[0][:, None]
    gain_imag = transmit[1][:, None]
    shaped_real = gain_real * spec_real - gain_imag * spec_imag
    shaped_imag = gain_real * spec_imag + gain_imag * spec_real
    back_real = (matmul(cosine, shaped_real) - matmul(sine_part, shaped_imag)) / total_slices
    back_imag = (matmul(cosine, shaped_imag) + matmul(sine_part, shaped_real)) / total_slices
    back_parts = jnp.stack([back_real, back_imag], axis=1)[:, :, None, :]
    returned = lax.all_to_all(back_parts, "cuts", split_axis=0, concat_axis=2, tiled=True)
    filtered = returned.reshape(members, 2, padded_span)[:, :, :pixel_span]
    filtered = filtered.reshape(members, 2, row_part, grid_size)
    restored = lax.all_to_all(filtered, "group", split_axis=0, concat_axis=2, tiled=True)
    return restored[0]


def on_device(radiation, phases, energy, pixels, destination, propagator, transmit):
    field_now = radiation[0]
    flat_phase = phases.reshape(-1)
    flat_energy = energy.reshape(-1)
    flat_pixel = pixels.reshape(-1)
    for step_index in range(STEPS):
        field_now, flat_phase, flat_energy = undulate(
            field_now, flat_phase, flat_energy, flat_pixel, propagator
        )
    field_now = crystal_filter(field_now, transmit)
    cut_count = lax.axis_size("cuts")
    block_count = destination.shape[1]
    block_size = phases.shape[-1]
    send_cap = max(2, 2 * block_count // cut_count)
    dest_row = destination[0]
    cut_ids = jnp.arange(cut_count, dtype=jnp.int32)
    match = (dest_row[:, None] == cut_ids[None, :]).astype(jnp.int32)
    earlier = jnp.cumsum(match, axis=0) - match
    rank_in = jnp.sum(match * earlier, axis=1)
    slot_ids = dest_row * send_cap + rank_in
    payload = jnp.stack(
        [
            flat_phase.reshape(block_count, block_size),
            flat_energy.reshape(block_count, block_size),
            flat_pixel.reshape(block_count, block_size).astype(jnp.float32),
        ],
        axis=1,
    )
    buffer = (
        jnp.zeros((cut_count * send_cap, 3, block_size), jnp.float32)
        .at[:, 2]
        .set(-1.0)
        .at[slot_ids]
        .set(payload)
    )
    moved = lax.all_to_all(
        buffer.reshape(cut_count, send_cap, 3, block_size),
        "cuts",
        split_axis=0,
        concat_axis=0,
        tiled=True,
    )
    moved = moved.reshape(cut_count * send_cap, 3, block_size)
    flat_phase = moved[:, 0].reshape(-1)
    flat_energy = moved[:, 1].reshape(-1)
    flat_pixel = moved[:, 2].reshape(-1).astype(jnp.int32)
    for step_index in range(STEPS):
        field_now, flat_phase, flat_energy = undulate(
            field_now, flat_phase, flat_energy, flat_pixel, propagator
        )
    return field_now[None]


def solution(mesh):
    return jax.shard_map(
        on_device,
        mesh=mesh,
        in_specs=(
            P(("cuts", "group"), None, None, None),
            P(("cuts", "group"), None, None),
            P(("cuts", "group"), None, None),
            P(("cuts", "group"), None, None),
            P(("cuts", "group"), None),
            P(),
            P(),
        ),
        out_specs=P(("cuts", "group"), None, None, None),
        check_vma=False,
    )
```

profile of v0, /device:TPU:8, one launch (start us, length us, event | category | flops | bytes accessed | tf_op | source)
XLA Modules:
  0.0 106.4 jit_solution(14722945761754793108)
XLA Ops:
  0.0 0.7 add_select_fusion.3
  0.7 0.9 bitcast_convert_fusion.3
  1.6 0.6 fusion.55
  2.9 0.9 fusion.37
  5.3 0.3 convolution_add_fusion.9
  6.2 1.9 %collective-permute-start = (f32[2,128,128]{2,1,0:T(8,128)S(1)}, f32[2,128,128]{2,1,0:T(8,128)S(1)}, u32[]{:S(2)}, u32[]{:S(2)}) collective-permute-start(f32[2,128,128]{2,1,0:T(8,128)S(1)} %pad_maximum_fusion), channel_id=1, source_target_pairs={{0,1},{1,2},{2,3},{3,4},{4,5},{5,6},{6,7},{7,8},{8,9},{9,10},{10,1... | collective-permute-start | bytes 393224 | tf_op jit(solution)/shard_map/ppermute | solution.py:19
  8.4 5.8 %collective-permute-done = f32[2,128,128]{2,1,0:T(8,128)S(1)} collective-permute-done((f32[2,128,128]{2,1,0:T(8,128)S(1)}, f32[2,128,128]{2,1,0:T(8,128)S(1)}, u32[]{:S(2)}, u32[]{:S(2)}) %collective-permute-start) | collective-permute-done | bytes 131104 | tf_op jit(solution)/shard_map/ppermute | solution.py:19
  14.3 0.6 fusion.53
  15.5 0.9 fusion.41
  16.7 0.3 convolution_subtract_fusion.7
  18.8 1.9 %collective-permute-start.1 = (f32[2,128,128]{2,1,0:T(8,128)S(1)}, f32[2,128,128]{2,1,0:T(8,128)S(1)}, u32[]{:S(2)}, u32[]{:S(2)}) collective-permute-start(f32[2,128,128]{2,1,0:T(8,128)S(1)} %pad_maximum_fusion.1), channel_id=1, source_target_pairs={{0,1},{1,2},{2,3},{3,4},{4,5},{5,6},{6,7},{7,8},{8,9},{9,10},{10,1... | collective-permute-start | bytes 393224 | tf_op jit(solution)/shard_map/ppermute | solution.py:19
  20.7 6.1 %collective-permute-done.1 = f32[2,128,128]{2,1,0:T(8,128)S(1)} collective-permute-done((f32[2,128,128]{2,1,0:T(8,128)S(1)}, f32[2,128,128]{2,1,0:T(8,128)S(1)}, u32[]{:S(2)}, u32[]{:S(2)}) %collective-permute-start.1) | collective-permute-done | bytes 131104 | tf_op jit(solution)/shard_map/ppermute | solution.py:19
  26.8 0.8 copy.22
  27.6 3.4 %all-to-all-start = ((f32[1,2,128,128]{3,1,0,2:T(2,128)}), f32[1,2,128,128]{3,1,0,2:T(2,128)S(1)}, u32[]{:S(2)}, u32[]{:S(2)}) async-start(f32[1,2,128,128]{3,1,0,2:T(2,128)} %copy.22), calls=%async_computation | async-start | bytes 262144 | tf_op jit(solution)/shard_map/all_to_all | solution.py:67
  31.1 1.0 scatter_fusion
  32.2 0.6 copy.29
  32.8 3.7 %all-to-all-done = f32[1,2,128,128]{3,1,0,2:T(2,128)S(1)} async-done(((f32[1,2,128,128]{3,1,0,2:T(2,128)}), f32[1,2,128,128]{3,1,0,2:T(2,128)S(1)}, u32[]{:S(2)}, u32[]{:S(2)}) %all-to-all-start) | async-done | bytes 131104 | tf_op jit(solution)/shard_map/all_to_all | solution.py:67
  36.4 5.3 %all-to-all-start.4 = ((f32[4,8,3,128]{3,1,2,0:T(8,128)}), f32[4,8,3,128]{3,1,2,0:T(8,128)S(1)}, u32[]{:S(2)}, u32[]{:S(2)}) async-start(f32[4,8,3,128]{3,1,2,0:T(8,128)} %copy.29), calls=%async_computation.4 | async-start | bytes 98304 | tf_op jit(solution)/shard_map/all_to_all | solution.py:138
  41.9 0.7 copy.24
  42.6 3.7 %all-to-all-done.4 = f32[4,8,3,128]{3,1,2,0:T(8,128)S(1)} async-done(((f32[4,8,3,128]{3,1,2,0:T(8,128)}), f32[4,8,3,128]{3,1,2,0:T(8,128)S(1)}, u32[]{:S(2)}, u32[]{:S(2)}) %all-to-all-start.4) | async-done | bytes 49184 | tf_op jit(solution)/shard_map/all_to_all | solution.py:138
  46.3 4.5 %all-to-all-start.1 = ((f32[8,2,4,512]{3,0,1,2:T(8,128)}), f32[8,2,4,512]{3,0,1,2:T(8,128)S(1)}, u32[]{:S(2)}, u32[]{:S(2)}) async-start(f32[8,2,4,512]{3,0,1,2:T(8,128)} %copy.24), calls=%async_computation.1 | async-start | bytes 262144 | tf_op jit(solution)/shard_map/all_to_all | solution.py:81
  50.8 5.2 %all-to-all-done.1 = f32[8,2,4,512]{3,0,1,2:T(8,128)S(1)} async-done(((f32[8,2,4,512]{3,0,1,2:T(8,128)}), f32[8,2,4,512]{3,0,1,2:T(8,128)S(1)}, u32[]{:S(2)}, u32[]{:S(2)}) %all-to-all-start.1) | async-done | bytes 131104 | tf_op jit(solution)/shard_map/all_to_all | solution.py:81
  57.1 0.3 fusion.174
  57.7 0.3 fusion.26
  57.9 0.3 fusion.28
  58.3 0.8 copy.26
  59.0 4.1 %all-to-all-start.2 = ((f32[32,2,1,512]{3,1,2,0:T(2,128)}), f32[32,2,1,512]{3,1,2,0:T(2,128)S(1)}, u32[]{:S(2)}, u32[]{:S(2)}) async-start(f32[32,2,1,512]{3,1,2,0:T(2,128)} %copy.26), calls=%async_computation.2 | async-start | bytes 262144 | tf_op jit(solution)/shard_map/all_to_all | solution.py:96
  63.1 5.1 %all-to-all-done.2 = f32[32,2,1,512]{3,1,2,0:T(2,128)S(1)} async-done(((f32[32,2,1,512]{3,1,2,0:T(2,128)}), f32[32,2,1,512]{3,1,2,0:T(2,128)S(1)}, u32[]{:S(2)}, u32[]{:S(2)}) %all-to-all-start.2) | async-done | bytes 131104 | tf_op jit(solution)/shard_map/all_to_all | solution.py:96
  68.3 0.7 reshape_reshape.4
  69.0 3.6 %all-to-all-start.3 = ((f32[8,2,16,128]{3,2,1,0:T(8,128)}), f32[8,2,16,128]{3,2,1,0:T(8,128)S(1)}, u32[]{:S(2)}, u32[]{:S(2)}) async-start(f32[8,2,16,128]{3,2,1,0:T(8,128)} %reshape_reshape.4), calls=%async_computation.3 | async-start | bytes 262144 | tf_op jit(solution)/shard_map/all_to_all | solution.py:99
  72.6 5.3 %all-to-all-done.3 = f32[8,2,16,128]{3,2,1,0:T(8,128)S(1)} async-done(((f32[8,2,16,128]{3,2,1,0:T(8,128)}), f32[8,2,16,128]{3,2,1,0:T(8,128)S(1)}, u32[]{:S(2)}, u32[]{:S(2)}) %all-to-all-start.3) | async-done | bytes 131104 | tf_op jit(solution)/shard_map/all_to_all | solution.py:99
  77.9 0.9 fusion.18
  78.8 0.5 fusion.3
  79.5 0.4 fusion.15
  79.9 1.5 %fusion.4 = f32[128,256]{1,0:T(8,128)S(1)} fusion(bf16[4096,128]{0,1:T(8,128)(2,1)S(1)} %get-tuple-element.52, bf16[4096,128]{0,1:T(8,128)(2,1)S(1)} %get-tuple-element.51, s32[4096]{0:T(1024)S(1)} %get-tuple-element.31), kind=kOutput, calls=%fused_computation.9 | convolution fusion | flops 273678336 | bytes 2244608 | tf_op jit(solution)/shard_map/dot_general | solution.py:50
  83.7 1.9 %collective-permute-start.2 = (f32[2,128,128]{2,1,0:T(8,128)S(1)}, f32[2,128,128]{2,1,0:T(8,128)S(1)}, u32[]{:S(2)}, u32[]{:S(2)}) collective-permute-start(f32[2,128,128]{2,1,0:T(8,128)S(1)} %pad_maximum_fusion.3), channel_id=1, source_target_pairs={{0,1},{1,2},{2,3},{3,4},{4,5},{5,6},{6,7},{7,8},{8,9},{9,10},{10,1... | collective-permute-start | bytes 393224 | tf_op jit(solution)/shard_map/ppermute | solution.py:19
  85.7 6.2 %collective-permute-done.2 = f32[2,128,128]{2,1,0:T(8,128)S(1)} collective-permute-done((f32[2,128,128]{2,1,0:T(8,128)S(1)}, f32[2,128,128]{2,1,0:T(8,128)S(1)}, u32[]{:S(2)}, u32[]{:S(2)}) %collective-permute-start.2) | collective-permute-done | bytes 131104 | tf_op jit(solution)/shard_map/ppermute | solution.py:19
  91.8 0.9 fusion.16
  92.7 0.5 fusion.1
  93.4 0.4 fusion.13
  93.8 1.5 %fusion.8 = f32[128,256]{1,0:T(8,128)S(1)} fusion(bf16[4096,128]{0,1:T(8,128)(2,1)S(1)} %get-tuple-element.50, bf16[4096,128]{0,1:T(8,128)(2,1)S(1)} %get-tuple-element.49, s32[4096]{0:T(1024)S(1)} %get-tuple-element.31), kind=kOutput, calls=%fused_computation.13 | convolution fusion | flops 273678336 | bytes 2244608 | tf_op jit(solution)/shard_map/dot_general | solution.py:50
  95.3 0.3 fusion.87
  95.6 0.3 convolution_subtract_fusion.1
  96.5 0.3 fusion.85
  96.8 0.3 convolution_add_fusion.1
  97.7 1.9 %collective-permute-start.3 = (f32[2,128,128]{2,1,0:T(8,128)S(1)}, f32[2,128,128]{2,1,0:T(8,128)S(1)}, u32[]{:S(2)}, u32[]{:S(2)}) collective-permute-start(f32[2,128,128]{2,1,0:T(8,128)S(1)} %pad_maximum_fusion.4), channel_id=1, source_target_pairs={{0,1},{1,2},{2,3},{3,4},{4,5},{5,6},{6,7},{7,8},{8,9},{9,10},{10,1... | collective-permute-start | bytes 393224 | tf_op jit(solution)/shard_map/ppermute | solution.py:19
  99.6 6.2 %collective-permute-done.3 = f32[2,128,128]{2,1,0:T(8,128)S(1)} collective-permute-done((f32[2,128,128]{2,1,0:T(8,128)S(1)}, f32[2,128,128]{2,1,0:T(8,128)S(1)}, u32[]{:S(2)}, u32[]{:S(2)}) %collective-permute-start.3) | collective-permute-done | bytes 131104 | tf_op jit(solution)/shard_map/ppermute | solution.py:19
  105.8 0.7 copy.41
  (88 shorter events, 11.2 us)
Async XLA Ops:
  1.6 0.9 copy-start.3
  1.6 0.9 copy-start.5
  2.5 1.3 %copy-start = (f32[2,128,128]{2,1,0:T(8,128)S(1)}, f32[2,128,128]{2,1,0:T(8,128)}, u32[]{:S(2)}) copy-start(f32[2,128,128]{2,1,0:T(8,128)} %param.14) | copy-start | bytes 393220
  2.5 1.3 %copy-start.1 = (f32[1,2,128,128]{3,2,1,0:T(8,128)S(1)}, f32[1,2,128,128]{3,2,1,0:T(8,128)}, u32[]{:S(2)}) copy-start(f32[1,2,128,128]{3,2,1,0:T(8,128)} %param.9) | copy-start | bytes 393220
  2.9 5.2 %copy-start.4 = (s32[1,16,128]{2,1,0:T(8,128)S(1)}, s32[1,16,128]{2,1,0:T(8,128)}, u32[]{:S(2)}) copy-start(s32[1,16,128]{2,1,0:T(8,128)} %param.12) | copy-start | bytes 24580
  2.9 5.3 %copy-start.6 = (s32[1,16]{1,0:T(1,128)S(1)}, s32[1,16]{1,0:T(1,128)}, u32[]{:S(2)}) copy-start(s32[1,16]{1,0:T(1,128)} %param.13) | copy-start | bytes 196
  6.2 8.1 %collective-permute-start = (f32[2,128,128]{2,1,0:T(8,128)S(1)}, f32[2,128,128]{2,1,0:T(8,128)S(1)}, u32[]{:S(2)}, u32[]{:S(2)}) collective-permute-start(f32[2,128,128]{2,1,0:T(8,128)S(1)} %pad_maximum_fusion), channel_id=1, source_target_pairs={{0,1},{1,2},{2,3},{3,4},{4,5},{5,6},{6,7},{7,8},{8,9},{9,10},{10,1... | collective-permute-start | bytes 393224 | tf_op jit(solution)/shard_map/ppermute | solution.py:19
  16.4 14.8 %copy-start.2 = (f32[32,3,128]{2,1,0:T(4,128)S(1)}, f32[32,3,128]{2,1,0:T(4,128)}, u32[]{:S(2)}) copy-start(f32[32,3,128]{2,1,0:T(4,128)} %constant.136.clone.1) | copy-start | bytes 147460
  17.3 33.5 %copy-start.7 = (f32[2,32]{1,0:T(2,128)S(1)}, f32[2,32]{1,0:T(2,128)}, u32[]{:S(2)}) copy-start(f32[2,32]{1,0:T(2,128)} %param.15) | copy-start | bytes 772
  18.8 8.1 %collective-permute-start.1 = (f32[2,128,128]{2,1,0:T(8,128)S(1)}, f32[2,128,128]{2,1,0:T(8,128)S(1)}, u32[]{:S(2)}, u32[]{:S(2)}) collective-permute-start(f32[2,128,128]{2,1,0:T(8,128)S(1)} %pad_maximum_fusion.1), channel_id=1, source_target_pairs={{0,1},{1,2},{2,3},{3,4},{4,5},{5,6},{6,7},{7,8},{8,9},{9,10},{10,1... | collective-permute-start | bytes 393224 | tf_op jit(solution)/shard_map/ppermute | solution.py:19
  27.6 8.8 %all-to-all-start = ((f32[1,2,128,128]{3,1,0,2:T(2,128)}), f32[1,2,128,128]{3,1,0,2:T(2,128)S(1)}, u32[]{:S(2)}, u32[]{:S(2)}) async-start(f32[1,2,128,128]{3,1,0,2:T(2,128)} %copy.22), calls=%async_computation | async-start | bytes 262144 | tf_op jit(solution)/shard_map/all_to_all | solution.py:67
  36.4 9.8 %all-to-all-start.4 = ((f32[4,8,3,128]{3,1,2,0:T(8,128)}), f32[4,8,3,128]{3,1,2,0:T(8,128)S(1)}, u32[]{:S(2)}, u32[]{:S(2)}) async-start(f32[4,8,3,128]{3,1,2,0:T(8,128)} %copy.29), calls=%async_computation.4 | async-start | bytes 98304 | tf_op jit(solution)/shard_map/all_to_all | solution.py:138
  46.3 9.7 %all-to-all-start.1 = ((f32[8,2,4,512]{3,0,1,2:T(8,128)}), f32[8,2,4,512]{3,0,1,2:T(8,128)S(1)}, u32[]{:S(2)}, u32[]{:S(2)}) async-start(f32[8,2,4,512]{3,0,1,2:T(8,128)} %copy.24), calls=%async_computation.1 | async-start | bytes 262144 | tf_op jit(solution)/shard_map/all_to_all | solution.py:81
  59.0 9.2 %all-to-all-start.2 = ((f32[32,2,1,512]{3,1,2,0:T(2,128)}), f32[32,2,1,512]{3,1,2,0:T(2,128)S(1)}, u32[]{:S(2)}, u32[]{:S(2)}) async-start(f32[32,2,1,512]{3,1,2,0:T(2,128)} %copy.26), calls=%async_computation.2 | async-start | bytes 262144 | tf_op jit(solution)/shard_map/all_to_all | solution.py:96
  69.0 8.8 %all-to-all-start.3 = ((f32[8,2,16,128]{3,2,1,0:T(8,128)}), f32[8,2,16,128]{3,2,1,0:T(8,128)S(1)}, u32[]{:S(2)}, u32[]{:S(2)}) async-start(f32[8,2,16,128]{3,2,1,0:T(8,128)} %reshape_reshape.4), calls=%async_computation.3 | async-start | bytes 262144 | tf_op jit(solution)/shard_map/all_to_all | solution.py:99
  83.7 8.1 %collective-permute-start.2 = (f32[2,128,128]{2,1,0:T(8,128)S(1)}, f32[2,128,128]{2,1,0:T(8,128)S(1)}, u32[]{:S(2)}, u32[]{:S(2)}) collective-permute-start(f32[2,128,128]{2,1,0:T(8,128)S(1)} %pad_maximum_fusion.3), channel_id=1, source_target_pairs={{0,1},{1,2},{2,3},{3,4},{4,5},{5,6},{6,7},{7,8},{8,9},{9,10},{10,1... | collective-permute-start | bytes 393224 | tf_op jit(solution)/shard_map/ppermute | solution.py:19
  97.7 8.1 %collective-permute-start.3 = (f32[2,128,128]{2,1,0:T(8,128)S(1)}, f32[2,128,128]{2,1,0:T(8,128)S(1)}, u32[]{:S(2)}, u32[]{:S(2)}) collective-permute-start(f32[2,128,128]{2,1,0:T(8,128)S(1)} %pad_maximum_fusion.4), channel_id=1, source_target_pairs={{0,1},{1,2},{2,3},{3,4},{4,5},{5,6},{6,7},{7,8},{8,9},{9,10},{10,1... | collective-permute-start | bytes 393224 | tf_op jit(solution)/shard_map/ppermute | solution.py:19
where the time goes:
time: 107 us; the launch traced here: 106 us
  waiting for transfers between devices  47.2 us (44%)
  starting transfers between devices  28.5 us (27%)
  matrix products  19.2 us (18%)
  local copies, waits for them, and re-layouts  6.38 us (6%)
  other arithmetic  4.48 us (4%)
    ppermute x4, waiting for transfers between devices, from_behind(): return lax.ppermute(block, axis, route)  24.3 us
    dot_general x40, matrix products, matmul(): jnp.dot(left, right, precision=lax.Precision.HIGHEST, preferred_element_t...  11.4 us
    ppermute x4, starting transfers between devices, from_behind(): return lax.ppermute(block, axis, route)  7.68 us
    all_to_all x1, starting transfers between devices, on_device(): lax.all_to_all(buffer.reshape(cut_count, send_cap, 3, block_size), 'cuts'...  5.32 us
    all_to_all x1, waiting for transfers between devices, crystal_filter(): lax.all_to_all(filtered, 'group', split_axis=0, concat_axis=2, tiled=True)  5.26 us
    all_to_all x1, waiting for transfers between devices, crystal_filter(): lax.all_to_all(stacked, 'cuts', split_axis=2, concat_axis=0, tiled=True)  5.15 us
    all_to_all x1, waiting for transfers between devices, crystal_filter(): lax.all_to_all(back_parts, 'cuts', split_axis=0, concat_axis=2, tiled=True)  5.15 us
    dot_general x4, matrix products, undulate(): lax.dot_general(row_hot, spread, (((0,), (0,)), ((), ())), preferred_elem...  4.77 us
  transfers between devices with their start and end apart: 9, of which 9 were waited for; matrix products, arithmetic and copies ran while one was open for 3% of the time, Pallas kernels for 0%

commit v1 on v0

v1 whole, which is shorter than its diff:
```python
import functools
import math

import jax
import jax.numpy as jnp
from jax import lax
from jax.experimental import pallas as pl
from jax.experimental.pallas import tpu as pltpu
from jax.sharding import PartitionSpec as P

STEPS = 2

KICK_RATE = 0.5
PHASE_RATE = 1.0
EMIT_RATE = 0.5

AXES = ("cuts", "group")
F32 = jnp.float32
BF16 = jnp.bfloat16
VMEM_LIMIT = 48 * 1024 * 1024


def dot(left, right, left_dim, right_dim):
    dims = (((left_dim,), (right_dim,)), ((), ()))
    return lax.dot_general(left, right, dims, preferred_element_type=F32)


def exact_dot(left, right):
    return jnp.dot(left, right, precision=lax.Precision.HIGHEST, preferred_element_type=F32)


def split(value):
    high = value.astype(BF16)
    return high, (value - high.astype(F32)).astype(BF16)


def diffract(real, imag, propagator):
    size = real.shape[0]
    prop_real, prop_imag = propagator[0], propagator[1]
    form = jnp.concatenate(
        [
            jnp.concatenate([prop_real, -prop_imag], axis=1),
            jnp.concatenate([prop_imag, prop_real], axis=1),
        ],
        axis=0,
    )
    form_high, form_low = split(form)
    high, low = split(jnp.concatenate([real, imag], axis=1))
    both = dot(jnp.concatenate([high, low], axis=0), form_high, 1, 1)
    right = both[:size] + both[size:] + dot(high, form_low, 1, 1)
    high, low = split(jnp.concatenate([right[:, :size], right[:, size:]], axis=0))
    both = dot(form_high, jnp.concatenate([high, low], axis=1), 1, 0)
    out = both[:, :size] + both[:, size:] + dot(form_low, high, 1, 0)
    return out[:size], out[size:]


def cells(pixels, grid):
    shift = grid.bit_length() - 1
    if grid == 1 << shift:
        return lax.shift_right_arithmetic(pixels, shift), pixels & (grid - 1)
    return pixels // grid, pixels % grid


def chunks(blocks):
    width = 2 if blocks % 2 == 0 else 1
    return [(start, width) for start in range(0, blocks, width)]


def lanes(array, start, width):
    return jnp.concatenate([array[start + k : start + k + 1] for k in range(width)], axis=1)


def hits(ids, grid):
    return lax.broadcasted_iota(jnp.int32, (grid, ids.shape[1]), 0) == ids


def kick(real, imag, phases, energy, pixels, read_ref):
    grid = real.shape[0]
    blocks, size = phases.shape
    low = jnp.concatenate([real, imag], axis=1).astype(BF16)
    row, col = cells(pixels, grid)
    for start, width in chunks(blocks):
        row_hot = jnp.where(hits(lanes(row, start, width), grid), 1.0, 0.0).astype(BF16)
        picked = dot(low, row_hot, 0, 0)
        col_hit = hits(lanes(col, start, width), grid)
        for part in range(2):
            value = picked[part * grid : (part + 1) * grid]
            value = jnp.sum(jnp.where(col_hit, value, 0.0), axis=0, keepdims=True)
            for k in range(width):
                read_ref[part, start + k : start + k + 1, :] = value[:, k * size : (k + 1) * size]
    read_real = read_ref[0, :blocks, :]
    read_imag = read_ref[1, :blocks, :]
    energy = energy - KICK_RATE * (read_real * jnp.cos(phases) - read_imag * jnp.sin(phases))
    return phases + PHASE_RATE * energy, energy


def emit(real, imag, phases, pixels, row_ref, spread_ref):
    grid = real.shape[0]
    blocks, size = phases.shape
    row, col = cells(pixels, grid)
    weight_real = jnp.cos(phases)
    weight_imag = -jnp.sin(phases)
    for start, width in chunks(blocks):
        where = pl.ds(start * size, width * size)
        row_ref[:, where] = jnp.where(hits(lanes(row, start, width), grid), 1.0, 0.0).astype(BF16)
        col_hit = hits(lanes(col, start, width), grid)
        for part, weight in ((0, weight_real), (1, weight_imag)):
            value = jnp.where(col_hit, lanes(weight, start, width), 0.0)
            spread_ref[part * grid : (part + 1) * grid, where] = value.astype(BF16)
    span = blocks * size
    source = dot(row_ref[:, :span], spread_ref[:, :span], 1, 1)
    return real + EMIT_RATE * source[:, :grid], imag + EMIT_RATE * source[:, grid:]


def position():
    return lax.axis_index("cuts") * lax.axis_size("group") + lax.axis_index("group")


def kept_unless(index):
    return jnp.where(position() == index, 0.0, 1.0).astype(F32)


def kick_kernel(field, phases, energy, pixels, out, read_ref):
    blocks = phases.shape[0]
    new_phases, new_energy = kick(field[0], field[1], phases[...], energy[...], pixels[...], read_ref)
    out[0:blocks, :] = new_phases
    out[blocks : 2 * blocks, :] = new_energy
    out[2 * blocks : 3 * blocks, :] = pixels[...].astype(F32)


def radiate_kernel(count, field, state, propagator, out, row_ref, spread_ref):
    blocks = state.shape[0] // 3
    pixels = state[2 * blocks : 3 * blocks, :].astype(jnp.int32)
    real, imag = emit(field[0], field[1], state[0:blocks, :], pixels, row_ref, spread_ref)
    real, imag = diffract(real, imag, propagator)
    keep = kept_unless(count - 1)
    out[0] = real * keep
    out[1] = imag * keep


def second_kernel(count, rows, field, state, propagator, out, state_out, read_ref, row_ref, spread_ref):
    blocks = state.shape[0] // 3
    real, imag = field[0], field[1]
    grid = real.shape[0]
    pixels = state[2 * blocks : 3 * blocks, :].astype(jnp.int32)
    phases, energy = kick(real, imag, state[0:blocks, :], state[blocks : 2 * blocks, :], pixels, read_ref)
    state_out[0:blocks, :] = phases
    state_out[blocks : 2 * blocks, :] = energy
    state_out[2 * blocks : 3 * blocks, :] = state[2 * blocks : 3 * blocks, :]
    real, imag = emit(real, imag, phases, pixels, row_ref, spread_ref)
    real, imag = diffract(real, imag, propagator)
    keep = kept_unless(count - 2)
    real, imag = real * keep, imag * keep
    if rows:
        for part in range(grid // rows):
            out[part, 0:rows, :] = real[part * rows : (part + 1) * rows]
            out[part, rows : 2 * rows, :] = imag[part * rows : (part + 1) * rows]
    else:
        out[0] = real
        out[1] = imag


def matrix_kernel(transmit, cos_out, sin_out, cos_in, sin_in, out):
    count = cos_in.shape[0]
    gain_real, gain_imag = transmit[0:1, :], transmit[1:2, :]
    for which in range(2):
        cosine, sine = cos_out[which], sin_out[which]
        real = cosine * gain_real - sine * gain_imag
        imag = cosine * gain_imag + sine * gain_real
        full_real = exact_dot(real, cos_in[...]) + exact_dot(imag, sin_in[...])
        full_imag = exact_dot(imag, cos_in[...]) - exact_dot(real, sin_in[...])
        base = 2 * which * count
        out[base : base + count, :] = jnp.concatenate([full_real, -full_imag], axis=1)
        out[base + count : base + 2 * count, :] = jnp.concatenate([full_imag, full_real], axis=1)


def filter_kernel(rows, matrix, data, out):
    count = data.shape[0] // (2 * rows)
    size = data.shape[1]
    stacked = jnp.concatenate(
        [
            jnp.concatenate(
                [data[pl.ds(part * rows + j, count, stride=2 * rows), :] for part in range(2)], axis=0
            )
            for j in range(rows)
        ],
        axis=1,
    )
    result = exact_dot(matrix[...], stacked)
    for kind in range(4):
        for j in range(rows):
            out[pl.ds(kind * rows + j, count, stride=4 * rows), :] = result[
                kind * count : (kind + 1) * count, j * size : (j + 1) * size
            ]


def pick_kernel(cuts, groups, cap, near, destination, states, out, buffer, slots, sems):
    total = cuts * groups
    blocks = buffer.shape[2] // 3
    me = position()
    copies = []
    homes = []
    for which in range(2):
        home = lax.rem(me + (total - 2 + which), total)
        homes.append(home)
        for cut in range(cuts):
            source = cut * groups + lax.rem(home, groups)
            if near:
                held = states.at[lax.div(lax.rem(source + 2 - which, total), groups), which]
            else:
                held = states.at[lax.rem(source + total - 1, total)]
            copy = pltpu.make_async_copy(held, buffer.at[which, cut], sems.at[which, cut])
            copy.start()
            copies.append(copy)
    for copy in copies:
        copy.wait()
    capacity = cuts * cap
    for which in range(2):
        home = homes[which]
        wanted = lax.div(home, groups)
        place = lax.rem(home, groups)
        used = 0
        for cut in range(cuts):
            for block in range(blocks):
                for kind in range(3):
                    slots[which, kind, pl.ds(used, 1), :] = buffer[
                        which, cut, kind * blocks + block : kind * blocks + block + 1, :
                    ]
                goes = destination[(cut * groups + place) * blocks + block] == wanted
                used = used + jnp.where(goes, 1, 0)
        filled = lax.broadcasted_iota(jnp.int32, (capacity, out.shape[3]), 0) < used
        for kind, empty in ((0, 0.0), (1, 0.0), (2, -1.0)):
            out[which, kind] = jnp.where(filled, slots[which, kind, 0:capacity, :], empty)


def last_kernel(rows, fields, state, propagator, out, field_ref, read_ref, row_ref, spread_ref):
    grid = propagator.shape[1]
    if rows:
        for part in range(grid // rows):
            for kind in range(4):
                field_ref[kind, part * rows : (part + 1) * rows, :] = fields[
                    part, kind * rows : (kind + 1) * rows, :
                ]
    else:
        for kind in range(4):
            field_ref[kind] = fields[kind]
    first_pixels = state[0, 2].astype(jnp.int32)
    next_pixels = state[1, 2].astype(jnp.int32)
    real, imag = field_ref[0], field_ref[1]
    phases, _ = kick(real, imag, state[0, 0], state[0, 1], first_pixels, read_ref.at[0])
    real, imag = emit(real, imag, phases, first_pixels, row_ref, spread_ref)
    phases, energy = kick(field_ref[2], field_ref[3], state[1, 0], state[1, 1], next_pixels, read_ref.at[1])
    real, imag = diffract(real, imag, propagator)
    keep = kept_unless(1)
    real, imag = real * keep, imag * keep
    phases, _ = kick(real, imag, phases, energy, next_pixels, read_ref.at[0])
    real, imag = emit(real, imag, phases, next_pixels, row_ref, spread_ref)
    real, imag = diffract(real, imag, propagator)
    keep = kept_unless(0)
    out[0] = real * keep
    out[1] = imag * keep


def call(kernel, out_shape, scratch, flops, args, memory=None):
    memory = memory or {}
    specs = [pl.BlockSpec(memory_space=memory.get(k, pltpu.VMEM)) for k in range(len(args))]
    return pl.pallas_call(
        kernel,
        out_shape=out_shape,
        in_specs=specs,
        out_specs=jax.tree.map(lambda _: pl.BlockSpec(memory_space=pltpu.VMEM), out_shape),
        scratch_shapes=scratch,
        compiler_params=pltpu.CompilerParams(vmem_limit_bytes=VMEM_LIMIT),
        cost_estimate=pl.CostEstimate(flops=flops, bytes_accessed=1 << 19, transcendentals=0),
    )(*args)


def time_tables(count):
    times = jnp.arange(count, dtype=jnp.int32)
    outs = [angle_table((times + (count - lag)) % count, times, count) for lag in (4, 3)]
    cos_out = jnp.stack([cosine for cosine, _ in outs]) / count
    sin_out = jnp.stack([sine for _, sine in outs]) / count
    return (cos_out, sin_out, *angle_table(times, times, count))


def angle_table(first_ids, second_ids, total_slices):
    product = first_ids[:, None] * second_ids[None, :] % total_slices
    angle = product.astype(F32) * (2.0 * math.pi / total_slices)
    return jnp.cos(angle), jnp.sin(angle)


def filter_any(field, transmit, count):
    grid = field.shape[1]
    span = grid * grid
    share = -(-span // count)
    flat = jnp.pad(field.reshape(2, span), ((0, 0), (0, share * count - span)))
    parts = flat.reshape(2, count, share).transpose(1, 0, 2)
    got = lax.all_to_all(parts, AXES, split_axis=0, concat_axis=0, tiled=True)
    got = jnp.roll(got, 2, axis=0)
    real, imag = got[:, 0], got[:, 1]
    times = jnp.arange(count, dtype=jnp.int32)
    cosine, sine = angle_table(times, times, count)
    spec_real = exact_dot(cosine, real) + exact_dot(sine, imag)
    spec_imag = exact_dot(cosine, imag) - exact_dot(sine, real)
    gain_real, gain_imag = transmit[0][:, None], transmit[1][:, None]
    shaped_real = gain_real * spec_real - gain_imag * spec_imag
    shaped_imag = gain_real * spec_imag + gain_imag * spec_real
    back_real = (exact_dot(cosine, shaped_real) - exact_dot(sine, shaped_imag)) / count
    back_imag = (exact_dot(cosine, shaped_imag) + exact_dot(sine, shaped_real)) / count
    back = jnp.stack([back_real, back_imag], axis=1)
    sent = jnp.stack([jnp.roll(back, 2, axis=0), jnp.roll(back, 1, axis=0)], axis=1)
    fields = lax.all_to_all(sent, AXES, split_axis=0, concat_axis=0, tiled=True)
    fields = fields.transpose(1, 2, 0, 3).reshape(4, share * count)[:, :span]
    return fields.reshape(4, grid, grid)


def on_device(radiation, phases, energy, pixels, destination, propagator, transmit):
    cuts, groups = lax.axis_size("cuts"), lax.axis_size("group")
    count = cuts * groups
    grid = radiation.shape[-1]
    blocks, size = phases.shape[1:]
    cap = max(2, 2 * blocks // cuts)
    rows = grid // count if grid % count == 0 and (2 * grid // count) % 8 == 0 else 0
    field = radiation[0]
    shape = lambda *dims: jax.ShapeDtypeStruct(dims, F32)
    read = lambda number: pltpu.VMEM((2, number, size), F32)
    hot = lambda number: [pltpu.VMEM((grid, number * size), BF16), pltpu.VMEM((2 * grid, number * size), BF16)]
    pass_flops = 4 * blocks * size * grid * grid
    prop_flops = 48 * grid**3

    everywhere = lax.all_gather(destination[0], AXES, tiled=True)
    state = call(
        kick_kernel, shape(3 * blocks, size), [read(blocks)], pass_flops,
        (field, phases[0], energy[0], pixels[0]),
    )
    route = [((i + 1) % count, i) for i in range(count)]
    behind = lax.ppermute(state, AXES, route)
    field = call(
        functools.partial(radiate_kernel, count), shape(2, grid, grid), hot(blocks), pass_flops + prop_flops,
        (field, state, propagator),
    )
    part_shape = shape(count, 2 * rows, grid) if rows else shape(2, grid, grid)
    field, state = call(
        functools.partial(second_kernel, count, rows), (part_shape, shape(3 * blocks, size)),
        [read(blocks)] + hot(blocks), 2 * pass_flops + prop_flops,
        (field, behind, propagator),
    )
    if rows:
        matrix = call(
            matrix_kernel, shape(4 * count, 2 * count), [], 1 << 20, (transmit, *time_tables(count))
        )
        data = lax.all_to_all(field, AXES, split_axis=0, concat_axis=0, tiled=True)
        states = lax.all_gather(state, AXES)
        sent = call(
            functools.partial(filter_kernel, rows), shape(count * 4 * rows, grid), [], 1 << 24,
            (matrix, data.reshape(count * 2 * rows, grid)),
        )
        fields = lax.all_to_all(
            sent.reshape(count, 4 * rows, grid), AXES, split_axis=0, concat_axis=0, tiled=True
        )
    else:
        shifted = [
            lax.ppermute(state, AXES, [(i, (i + ahead) % count) for i in range(count)]) for ahead in (3, 2)
        ]
        states = lax.all_gather(jnp.stack(shifted), "cuts")
        fields = filter_any(field, transmit, count)
    capacity = cuts * cap
    picked = call(
        functools.partial(pick_kernel, cuts, groups, cap, not rows), shape(2, 3, capacity, size),
        [
            pltpu.VMEM((2, cuts, 3 * blocks, size), F32),
            pltpu.VMEM((2, 3, capacity + 8, size), F32),
            pltpu.SemaphoreType.DMA((2, cuts)),
        ],
        1 << 20, (everywhere, states), {0: pltpu.SMEM, 1: pl.ANY},
    )
    out = call(
        functools.partial(last_kernel, rows), shape(2, grid, grid),
        [pltpu.VMEM((4, grid, grid), F32), pltpu.VMEM((2, 2, capacity, size), F32)] + hot(capacity),
        10 * pass_flops + 2 * prop_flops, (fields, picked, propagator),
    )
    return out[None]


def solution(mesh):
    return jax.shard_map(
        on_device,
        mesh=mesh,
        in_specs=(
            P(("cuts", "group"), None, None, None),
            P(("cuts", "group"), None, None),
            P(("cuts", "group"), None, None),
            P(("cuts", "group"), None, None),
            P(("cuts", "group"), None),
            P(),
            P(),
        ),
        out_specs=P(("cuts", "group"), None, None, None),
        check_vma=False,
    )
```

time: 107 us -> 123 us (1.15)
  the two profiles are of different devices: /device:TPU:8 before, /device:TPU:1 now
where the time goes in v1:
time: 123 us; the launch traced here: 122 us
  blocking collectives  83.2 us (68%)
  Pallas kernels  12.5 us (10%)
  starting transfers between devices  11.9 us (10%)
  waiting for transfers between devices  9.66 us (8%)
  local copies, waits for them, and re-layouts  4.43 us (4%)
    all_gather x1, blocking collectives, on_device(): states = lax.all_gather(state, AXES)  43.7 us
    all_gather x1, blocking collectives, on_device(): everywhere = lax.all_gather(destination[0], AXES, tiled=True)  39.5 us
    pallas_call x7, Pallas kernels, call(): pl.pallas_call(kernel, out_shape=out_shape, in_specs=specs, out_specs=jax...  12.5 us
    all_to_all x1, starting transfers between devices, on_device(): data = lax.all_to_all(field, AXES, split_axis=0, concat_axis=0, tiled=True)  9.27 us
    all_to_all x1, waiting for transfers between devices, on_device(): data = lax.all_to_all(field, AXES, split_axis=0, concat_axis=0, tiled=True)  6.89 us
    unnamed x16, local copies, waits for them, and re-layouts  4.43 us
    ppermute x1, waiting for transfers between devices, on_device(): behind = lax.ppermute(state, AXES, route)  2.77 us
    all_to_all x1, starting transfers between devices, on_device(): lax.all_to_all(sent.reshape(count, 4 * rows, grid), AXES, split_axis=0, c...  2.48 us
  transfers between devices with their start and end apart: 3, of which 2 were waited for; matrix products, arithmetic and copies ran while one was open for 0% of the time, Pallas kernels for 2%

profile of v1, /device:TPU:1, one launch (start us, length us, event | category | flops | bytes accessed | tf_op | source)
XLA Modules:
  0.0 122.2 jit_solution(7811228374341647994)
XLA Ops:
  0.0 0.0 copy-start.1
  0.0 0.9 copy-done.1
  0.9 0.0 copy-start.3
  0.9 0.7 copy-done.3
  1.6 0.0 copy-start.4
  1.6 0.7 copy-done.4
  2.3 0.0 copy-start.5
  2.3 0.7 copy-done.5
  3.0 0.0 copy-start.2
  3.0 0.6 shard_map.74.state
  3.6 0.1 collective-permute-start
  3.7 0.2 fusion.20
  3.9 0.0 copy-done.2
  3.9 1.1 shard_map.75.field
  5.0 2.8 %collective-permute-done.state = f32[48,128]{1,0:T(8,128)S(1)} collective-permute-done((f32[48,128]{1,0:T(8,128)S(1)}, f32[48,128]{1,0:T(8,128)S(1)}, u32[]{:S(2)}, u32[]{:S(2)}) %collective-permute-start) | collective-permute-done | bytes 24608 | tf_op jit(solution)/shard_map/ppermute | solution.py:337
  7.8 2.4 %shard_map.76 = (f32[32,8,128]{2,1,0:T(8,128)}, f32[48,128]{1,0:T(8,128)S(1)}) custom-call(f32[2,128,128]{2,1,0:T(8,128)S(1)} %shard_map.75.field, f32[48,128]{1,0:T(8,128)S(1)} %collective-permute-done.state, f32[2,128,128]{2,1,0:T(8,128)S(1)} %copy-done.2), custom_call_target="tpu_custom_call" | custom-call | flops 369098752 | bytes 524288 | tf_op jit(solution)/shard_map/pallas_call | solution.py:267
  10.2 9.3 %all-to-all-start = ((f32[32,8,128]{2,1,0:T(8,128)}), f32[32,8,128]{2,1,0:T(8,128)S(1)}, u32[]{:S(2)}, u32[]{:S(2)}) async-start(f32[32,8,128]{2,1,0:T(8,128)} %get-tuple-element.7), calls=%async_computation | async-start | bytes 262144 | tf_op jit(solution)/shard_map/all_to_all | solution.py:352
  19.4 0.2 fusion.22
  19.6 0.1 fusion.18
  19.7 0.0 copy-start
  19.7 0.7 copy-done
  20.4 0.4 shard_map.73.matrix
  20.8 6.9 %all-to-all-done = f32[32,8,128]{2,1,0:T(8,128)S(1)} async-done(((f32[32,8,128]{2,1,0:T(8,128)}), f32[32,8,128]{2,1,0:T(8,128)S(1)}, u32[]{:S(2)}, u32[]{:S(2)}) %all-to-all-start) | async-done | bytes 131104 | tf_op jit(solution)/shard_map/all_to_all | solution.py:352
  27.6 1.1 shard_map.77
  28.8 2.5 %all-to-all-start.1 = ((f32[32,16,128]{2,1,0:T(8,128)}), f32[32,16,128]{2,1,0:T(8,128)S(1)}, u32[]{:S(2)}, u32[]{:S(2)}) async-start(f32[32,16,128]{2,1,0:T(8,128)} %bitcast.5), calls=%async_computation.1 | async-start | bytes 524288 | tf_op jit(solution)/shard_map/all_to_all | solution.py:358
  31.3 0.0 copy-start.6
  31.3 0.6 copy-done.6
  31.9 0.1 bitcast_dynamic-update-slice_fusion
  32.0 39.5 %all-reduce.destination = s32[512]{0:T(512)S(1)} all-reduce(s32[512]{0:T(512)S(1)} %bitcast_dynamic-update-slice_fusion), channel_id=2, replica_groups=mesh['cuts'=4,'group'=8] {'cuts','group'}, use_global_device_ids=true, to_apply=%add | all-reduce | flops 512 | bytes 4096 | tf_op jit(solution)/shard_map/all_gather | solution.py:331
  71.5 43.7 %all-gather.1 = f32[1536,128]{1,0:T(8,128)S(1)} all-gather(f32[48,128]{1,0:T(8,128)S(1)} %get-tuple-element.8), channel_id=3, replica_groups=mesh['cuts'=4,'group'=8] {'cuts','group'}, dimensions={0}, use_global_device_ids=true | all-gather | bytes 811008 | tf_op jit(solution)/shard_map/all_gather | solution.py:353
  115.2 1.2 shard_map.78.state
  116.4 0.0 all-to-all-done.1.fields
  116.4 5.8 %shard_map.79 = f32[2,128,128]{2,1,0:T(8,128)} custom-call(f32[32,16,128]{2,1,0:T(8,128)S(1)} %all-to-all-done.1.fields, f32[2,3,32,128]{3,2,1,0:T(8,128)S(1)} %shard_map.78.state, f32[2,128,128]{2,1,0:T(8,128)S(1)} %copy-done.2), custom_call_target="tpu_custom_call" | custom-call | flops 1543503872 | bytes 524288 | tf_op jit(solution)/shard_map/pallas_call | solution.py:267
  (4 shorter events, 0.0 us)
Async XLA Ops:
  0.0 0.9 copy-start.1
  0.9 0.7 copy-start.3
  1.6 0.7 copy-start.4
  2.3 0.7 copy-start.5
  3.0 0.9 copy-start.2
  3.6 4.2 %collective-permute-start = (f32[48,128]{1,0:T(8,128)S(1)}, f32[48,128]{1,0:T(8,128)S(1)}, u32[]{:S(2)}, u32[]{:S(2)}) collective-permute-start(f32[48,128]{1,0:T(8,128)S(1)} %shard_map.74.state), channel_id=1, source_target_pairs={{1,0},{2,1},{3,2},{4,3},{5,4},{6,5},{7,6},{8,7},{9,8},{10,9},{11,1... | collective-permute-start | bytes 73736 | tf_op jit(solution)/shard_map/ppermute | solution.py:337
  10.2 17.5 %all-to-all-start = ((f32[32,8,128]{2,1,0:T(8,128)}), f32[32,8,128]{2,1,0:T(8,128)S(1)}, u32[]{:S(2)}, u32[]{:S(2)}) async-start(f32[32,8,128]{2,1,0:T(8,128)} %get-tuple-element.7), calls=%async_computation | async-start | bytes 262144 | tf_op jit(solution)/shard_map/all_to_all | solution.py:352
  19.7 0.7 copy-start
  28.8 87.7 %all-to-all-start.1 = ((f32[32,16,128]{2,1,0:T(8,128)}), f32[32,16,128]{2,1,0:T(8,128)S(1)}, u32[]{:S(2)}, u32[]{:S(2)}) async-start(f32[32,16,128]{2,1,0:T(8,128)} %bitcast.5), calls=%async_computation.1 | async-start | bytes 524288 | tf_op jit(solution)/shard_map/all_to_all | solution.py:358
  31.3 0.7 copy-start.6

commit v2 on v1

--- a/solution.py
+++ b/solution.py
@@ -8,8 +8,6 @@
 from jax.experimental.pallas import tpu as pltpu
 from jax.sharding import PartitionSpec as P
 
-STEPS = 2
-
 KICK_RATE = 0.5
 PHASE_RATE = 1.0
 EMIT_RATE = 0.5
@@ -18,6 +16,7 @@
 F32 = jnp.float32
 BF16 = jnp.bfloat16
 VMEM_LIMIT = 48 * 1024 * 1024
+WHOLE_VMEM = 60 * 1024 * 1024
 
 
 def dot(left, right, left_dim, right_dim):
@@ -120,16 +119,32 @@
     return jnp.where(position() == index, 0.0, 1.0).astype(F32)
 
 
-def kick_kernel(field, phases, energy, pixels, out, read_ref):
+def kick_kernel(field_hbm, phases_hbm, energy_hbm, pixels_hbm, dest_hbm, out, field, phases, energy, pixels, dest, read_ref, sems):
     blocks = phases.shape[0]
+    pairs = ((dest_hbm, dest), (field_hbm, field), (pixels_hbm, pixels), (phases_hbm, phases), (energy_hbm, energy))
+    copies = [pltpu.make_async_copy(source, target, sems.at[k]) for k, (source, target) in enumerate(pairs)]
+    for copy in copies:
+        copy.start()
+    for copy in copies:
+        copy.wait()
     new_phases, new_energy = kick(field[0], field[1], phases[...], energy[...], pixels[...], read_ref)
-    out[0:blocks, :] = new_phases
-    out[blocks : 2 * blocks, :] = new_energy
-    out[2 * blocks : 3 * blocks, :] = pixels[...].astype(F32)
+    goals = [dest[0, block] for block in range(blocks)]
+    ranks = [0] * blocks
+    for later in range(blocks):
+        for earlier in range(later):
+            first = (goals[earlier] <= goals[later]).astype(jnp.int32)
+            ranks[later] = ranks[later] + first
+            ranks[earlier] = ranks[earlier] + (1 - first)
+    whole = pixels[...].astype(F32)
+    for block in range(blocks):
+        for kind, value in enumerate((new_phases, new_energy, whole)):
+            out[pl.ds(kind * blocks + ranks[block], 1), :] = value[block : block + 1, :]
+        goal = jnp.full((1, out.shape[1]), goals[block].astype(F32), F32)
+        out[pl.ds(3 * blocks + ranks[block], 1), :] = goal
 
 
 def radiate_kernel(count, field, state, propagator, out, row_ref, spread_ref):
-    blocks = state.shape[0] // 3
+    blocks = state.shape[0] // 4
     pixels = state[2 * blocks : 3 * blocks, :].astype(jnp.int32)
     real, imag = emit(field[0], field[1], state[0:blocks, :], pixels, row_ref, spread_ref)
     real, imag = diffract(real, imag, propagator)
@@ -138,15 +153,26 @@
     out[1] = imag * keep
 
 
-def second_kernel(count, rows, field, state, propagator, out, state_out, read_ref, row_ref, spread_ref):
-    blocks = state.shape[0] // 3
+def second_kernel(count, rows, cap, field, state, propagator, out, *rest):
+    sends = rest[:-3]
+    read_ref, row_ref, spread_ref = rest[-3:]
+    blocks = state.shape[0] // 4
     real, imag = field[0], field[1]
     grid = real.shape[0]
     pixels = state[2 * blocks : 3 * blocks, :].astype(jnp.int32)
     phases, energy = kick(real, imag, state[0:blocks, :], state[blocks : 2 * blocks, :], pixels, read_ref)
-    state_out[0:blocks, :] = phases
-    state_out[blocks : 2 * blocks, :] = energy
-    state_out[2 * blocks : 3 * blocks, :] = state[2 * blocks : 3 * blocks, :]
+    cuts = len(sends)
+    source = lax.rem(position() + 1, count)
+    cut = lax.div(source, count // cuts)
+    kinds = (phases, energy, state[2 * blocks : 3 * blocks, :])
+    for ahead, send in enumerate(sends):
+        wanted = lax.rem(cut + ahead, cuts).astype(F32)
+        chunk = [jnp.zeros((cap, phases.shape[1]), F32)] * 2 + [jnp.full((cap, phases.shape[1]), -1.0, F32)]
+        for start in range(0, blocks, cap):
+            goes = state[3 * blocks + start : 3 * blocks + start + cap, :] == wanted
+            chunk = [jnp.where(goes, kind[start : start + cap], old) for kind, old in zip(kinds, chunk)]
+        for kind in range(3):
+            send[kind * cap : (kind + 1) * cap, :] = chunk[kind]
     real, imag = emit(real, imag, phases, pixels, row_ref, spread_ref)
     real, imag = diffract(real, imag, propagator)
     keep = kept_unless(count - 2)
@@ -170,8 +196,15 @@
         full_real = exact_dot(real, cos_in[...]) + exact_dot(imag, sin_in[...])
         full_imag = exact_dot(imag, cos_in[...]) - exact_dot(real, sin_in[...])
         base = 2 * which * count
-        out[base : base + count, :] = jnp.concatenate([full_real, -full_imag], axis=1)
-        out[base + count : base + 2 * count, :] = jnp.concatenate([full_imag, full_real], axis=1)
+        form = jnp.concatenate(
+            [
+                jnp.concatenate([full_real, -full_imag], axis=1),
+                jnp.concatenate([full_imag, full_real], axis=1),
+            ],
+            axis=0,
+        )
+        high, low = split(form)
+        out[base : base + 2 * count, :] = jnp.concatenate([high, high, low], axis=1)
 
 
 def filter_kernel(rows, matrix, data, out):
@@ -186,7 +219,8 @@
         ],
         axis=1,
     )
-    result = exact_dot(matrix[...], stacked)
+    high, low = split(stacked)
+    result = dot(matrix[...], jnp.concatenate([high, low, high], axis=0), 1, 0)
     for kind in range(4):
         for j in range(rows):
             out[pl.ds(kind * rows + j, count, stride=4 * rows), :] = result[
@@ -194,46 +228,20 @@
             ]
 
 
-def pick_kernel(cuts, groups, cap, near, destination, states, out, buffer, slots, sems):
-    total = cuts * groups
-    blocks = buffer.shape[2] // 3
-    me = position()
-    copies = []
-    homes = []
-    for which in range(2):
-        home = lax.rem(me + (total - 2 + which), total)
-        homes.append(home)
-        for cut in range(cuts):
-            source = cut * groups + lax.rem(home, groups)
-            if near:
-                held = states.at[lax.div(lax.rem(source + 2 - which, total), groups), which]
-            else:
-                held = states.at[lax.rem(source + total - 1, total)]
-            copy = pltpu.make_async_copy(held, buffer.at[which, cut], sems.at[which, cut])
-            copy.start()
-            copies.append(copy)
-    for copy in copies:
-        copy.wait()
-    capacity = cuts * cap
-    for which in range(2):
-        home = homes[which]
-        wanted = lax.div(home, groups)
-        place = lax.rem(home, groups)
-        used = 0
-        for cut in range(cuts):
-            for block in range(blocks):
-                for kind in range(3):
-                    slots[which, kind, pl.ds(used, 1), :] = buffer[
-                        which, cut, kind * blocks + block : kind * blocks + block + 1, :
-                    ]
-                goes = destination[(cut * groups + place) * blocks + block] == wanted
-                used = used + jnp.where(goes, 1, 0)
-        filled = lax.broadcasted_iota(jnp.int32, (capacity, out.shape[3]), 0) < used
-        for kind, empty in ((0, 0.0), (1, 0.0), (2, -1.0)):
-            out[which, kind] = jnp.where(filled, slots[which, kind, 0:capacity, :], empty)
-
-
-def last_kernel(rows, fields, state, propagator, out, field_ref, read_ref, row_ref, spread_ref):
+def joined(chunks_in):
+    cap = chunks_in[0].shape[0] // 3
+    kinds = [
+        jnp.concatenate([chunk[kind * cap : (kind + 1) * cap, :] for chunk in chunks_in], axis=0)
+        for kind in range(3)
+    ]
+    return kinds[0], kinds[1], kinds[2].astype(jnp.int32)
+
+
+def last_kernel(rows, fields, propagator, *rest):
+    out, field_ref, read_ref, row_ref, spread_ref = rest[-5:]
+    half = (len(rest) - 5) // 2
+    first_phases, first_energy, first_pixels = joined(rest[:half])
+    phases, energy, next_pixels = joined(rest[half : 2 * half])
     grid = propagator.shape[1]
     if rows:
         for part in range(grid // rows):
@@ -244,12 +252,10 @@
     else:
         for kind in range(4):
             field_ref[kind] = fields[kind]
-    first_pixels = state[0, 2].astype(jnp.int32)
-    next_pixels = state[1, 2].astype(jnp.int32)
     real, imag = field_ref[0], field_ref[1]
-    phases, _ = kick(real, imag, state[0, 0], state[0, 1], first_pixels, read_ref.at[0])
-    real, imag = emit(real, imag, phases, first_pixels, row_ref, spread_ref)
-    phases, energy = kick(field_ref[2], field_ref[3], state[1, 0], state[1, 1], next_pixels, read_ref.at[1])
+    first_phases, _ = kick(real, imag, first_phases, first_energy, first_pixels, read_ref.at[0])
+    real, imag = emit(real, imag, first_phases, first_pixels, row_ref, spread_ref)
+    phases, energy = kick(field_ref[2], field_ref[3], phases, energy, next_pixels, read_ref.at[1])
     real, imag = diffract(real, imag, propagator)
     keep = kept_unless(1)
     real, imag = real * keep, imag * keep
@@ -261,16 +267,15 @@
     out[1] = imag * keep
 
 
-def call(kernel, out_shape, scratch, flops, args, memory=None):
-    memory = memory or {}
-    specs = [pl.BlockSpec(memory_space=memory.get(k, pltpu.VMEM)) for k in range(len(args))]
+def call(kernel, out_shape, scratch, flops, args, memory=pltpu.VMEM, limit=VMEM_LIMIT):
+    specs = [pl.BlockSpec(memory_space=memory)] * len(args)
     return pl.pallas_call(
         kernel,
         out_shape=out_shape,
         in_specs=specs,
         out_specs=jax.tree.map(lambda _: pl.BlockSpec(memory_space=pltpu.VMEM), out_shape),
         scratch_shapes=scratch,
-        compiler_params=pltpu.CompilerParams(vmem_limit_bytes=VMEM_LIMIT),
+        compiler_params=pltpu.CompilerParams(vmem_limit_bytes=limit),
         cost_estimate=pl.CostEstimate(flops=flops, bytes_accessed=1 << 19, transcendentals=0),
     )(*args)
 
@@ -328,10 +333,18 @@
     pass_flops = 4 * blocks * size * grid * grid
     prop_flops = 48 * grid**3
 
-    everywhere = lax.all_gather(destination[0], AXES, tiled=True)
     state = call(
-        kick_kernel, shape(3 * blocks, size), [read(blocks)], pass_flops,
-        (field, phases[0], energy[0], pixels[0]),
+        kick_kernel, shape(4 * blocks, size),
+        [
+            pltpu.VMEM((2, grid, grid), F32),
+            pltpu.VMEM((blocks, size), F32),
+            pltpu.VMEM((blocks, size), F32),
+            pltpu.VMEM((blocks, size), jnp.int32),
+            pltpu.SMEM((1, blocks), jnp.int32),
+            read(blocks),
+            pltpu.SemaphoreType.DMA((5,)),
+        ],
+        pass_flops, (field, phases[0], energy[0], pixels[0], destination), pl.ANY, WHOLE_VMEM,
     )
     route = [((i + 1) % count, i) for i in range(count)]
     behind = lax.ppermute(state, AXES, route)
@@ -340,17 +353,22 @@
         (field, state, propagator),
     )
     part_shape = shape(count, 2 * rows, grid) if rows else shape(2, grid, grid)
-    field, state = call(
-        functools.partial(second_kernel, count, rows), (part_shape, shape(3 * blocks, size)),
+    field, *sends = call(
+        functools.partial(second_kernel, count, rows, cap), (part_shape, *[shape(3 * cap, size)] * cuts),
         [read(blocks)] + hot(blocks), 2 * pass_flops + prop_flops,
         (field, behind, propagator),
     )
+    chunks_in = [
+        lax.ppermute(send, AXES, [(i, (i + lag + groups * ahead) % count) for i in range(count)])
+        for lag in (3, 2)
+        for ahead, send in enumerate(sends)
+    ]
     if rows:
         matrix = call(
-            matrix_kernel, shape(4 * count, 2 * count), [], 1 << 20, (transmit, *time_tables(count))
+            matrix_kernel, jax.ShapeDtypeStruct((4 * count, 6 * count), BF16), [], 1 << 20,
+            (transmit, *time_tables(count)),
         )
         data = lax.all_to_all(field, AXES, split_axis=0, concat_axis=0, tiled=True)
-        states = lax.all_gather(state, AXES)
         sent = call(
             functools.partial(filter_kernel, rows), shape(count * 4 * rows, grid), [], 1 << 24,
             (matrix, data.reshape(count * 2 * rows, grid)),
@@ -359,25 +377,12 @@
             sent.reshape(count, 4 * rows, grid), AXES, split_axis=0, concat_axis=0, tiled=True
         )
     else:
-        shifted = [
-            lax.ppermute(state, AXES, [(i, (i + ahead) % count) for i in range(count)]) for ahead in (3, 2)
-        ]
-        states = lax.all_gather(jnp.stack(shifted), "cuts")
         fields = filter_any(field, transmit, count)
     capacity = cuts * cap
-    picked = call(
-        functools.partial(pick_kernel, cuts, groups, cap, not rows), shape(2, 3, capacity, size),
-        [
-            pltpu.VMEM((2, cuts, 3 * blocks, size), F32),
-            pltpu.VMEM((2, 3, capacity + 8, size), F32),
-            pltpu.SemaphoreType.DMA((2, cuts)),
-        ],
-        1 << 20, (everywhere, states), {0: pltpu.SMEM, 1: pl.ANY},
-    )
     out = call(
         functools.partial(last_kernel, rows), shape(2, grid, grid),
         [pltpu.VMEM((4, grid, grid), F32), pltpu.VMEM((2, 2, capacity, size), F32)] + hot(capacity),
-        10 * pass_flops + 2 * prop_flops, (fields, picked, propagator),
+        10 * pass_flops + 2 * prop_flops, (fields, propagator, *chunks_in),
     )
     return out[None]
 

time: 123 us -> 54.4 us (0.44)
  the two profiles are of different devices: /device:TPU:1 before, /device:TPU:0 now
where the time goes in v2:
time: 54.4 us; the launch traced here: 54.1 us
  starting transfers between devices  29.3 us (54%)
  Pallas kernels  12.9 us (24%)
  waiting for transfers between devices  10.7 us (20%)
  local copies, waits for them, and re-layouts  0.69 us (1%)
    ppermute x8, starting transfers between devices, on_device(): lax.ppermute(send, AXES, [(i, (i + lag + groups * ahead) % count) for i i...  14.7 us
    pallas_call x6, Pallas kernels, call(): pl.pallas_call(kernel, out_shape=out_shape, in_specs=specs, out_specs=jax...  12.9 us
    all_to_all x1, waiting for transfers between devices, on_device(): data = lax.all_to_all(field, AXES, split_axis=0, concat_axis=0, tiled=True)  6.85 us
    ppermute x1, starting transfers between devices, on_device(): behind = lax.ppermute(state, AXES, route)  6.42 us
    all_to_all x1, starting transfers between devices, on_device(): data = lax.all_to_all(field, AXES, split_axis=0, concat_axis=0, tiled=True)  5.59 us
    ppermute x8, waiting for transfers between devices, on_device(): lax.ppermute(send, AXES, [(i, (i + lag + groups * ahead) % count) for i i...  3.23 us
    all_to_all x1, starting transfers between devices, on_device(): lax.all_to_all(sent.reshape(count, 4 * rows, grid), AXES, split_axis=0, c...  2.58 us
  transfers between devices with their start and end apart: 11, of which 4 were waited for; matrix products, arithmetic and copies ran while one was open for 1% of the time, Pallas kernels for 3%

profile of v2, /device:TPU:0, one launch (start us, length us, event | category | flops | bytes accessed | tf_op | source)
XLA Modules:
  0.0 54.1 jit_solution(447725834082950948)
XLA Ops:
  0.0 0.0 copy-start.1
  0.0 0.0 copy-start.2
  0.0 2.2 %shard_map.74.state = f32[64,128]{1,0:T(8,128)} custom-call(f32[2,128,128]{2,1,0:T(8,128)} %bitcast.8, f32[16,128]{1,0:T(8,128)} %bitcast.10, f32[16,128]{1,0:T(8,128)} %bitcast.11, s32[16,128]{1,0:T(8,128)} %bitcast.12, s32[1,16]{1,0:T(1,128)} %dest_hbm.1), custom_call_target="tpu_custom_call" | custom-call | flops 134217728 | bytes 524288 | tf_op jit(solution)/shard_map/pallas_call | solution.py:272
  2.3 0.0 copy-start.3
  2.3 6.4 %collective-permute-start = (f32[64,128]{1,0:T(8,128)}, f32[64,128]{1,0:T(8,128)S(1)}, u32[]{:S(2)}, u32[]{:S(2)}) collective-permute-start(f32[64,128]{1,0:T(8,128)} %shard_map.74.state), channel_id=1, source_target_pairs={{1,0},{2,1},{3,2},{4,3},{5,4},{6,5},{7,6},{8,7},{9,8},{10,9},{11,1... | collective-permute-start | bytes 98312 | tf_op jit(solution)/shard_map/ppermute | solution.py:350
  8.7 0.2 fusion.22
  8.9 0.0 copy-done.1
  8.9 0.0 copy-done.2
  8.9 0.0 copy-done.3
  8.9 1.1 %shard_map.75.field = f32[2,128,128]{2,1,0:T(8,128)S(1)} custom-call(f32[2,128,128]{2,1,0:T(8,128)S(1)} %bitcast.9, f32[64,128]{1,0:T(8,128)S(1)} %copy-done.3, f32[2,128,128]{2,1,0:T(8,128)S(1)} %copy-done.2), custom_call_target="tpu_custom_call" | custom-call | flops 234881024 | bytes 524288 | tf_op jit(solution)/shard_map/pallas_call | solution.py:272
  10.0 0.6 %collective-permute-done.state = f32[64,128]{1,0:T(8,128)S(1)} collective-permute-done((f32[64,128]{1,0:T(8,128)}, f32[64,128]{1,0:T(8,128)S(1)}, u32[]{:S(2)}, u32[]{:S(2)}) %collective-permute-start) | collective-permute-done | bytes 32800 | tf_op jit(solution)/shard_map/ppermute | solution.py:350
  10.6 2.4 %shard_map.76 = (f32[32,8,128]{2,1,0:T(8,128)}, f32[24,128]{1,0:T(8,128)S(1)}, f32[24,128]{1,0:T(8,128)S(1)}, f32[24,128]{1,0:T(8,128)S(1)}, f32[24,128]{1,0:T(8,128)S(1)}) custom-call(f32[2,128,128]{2,1,0:T(8,128)S(1)} %shard_map.75.field, f32[64,128]{1,0:T(8,128)S(1)} %collective-permute-done.state, f32[2,128,128]{2,1,0:T(8,128)S(1)} %copy-done.2), custom_call_target="tpu_custom_call" | custom-call | flops 369098752 | bytes 524288 | tf_op jit(solution)/shard_map/pallas_call | solution.py:272
  13.0 5.6 %all-to-all-start = ((f32[32,8,128]{2,1,0:T(8,128)}), f32[32,8,128]{2,1,0:T(8,128)S(1)}, u32[]{:S(2)}, u32[]{:S(2)}) async-start(f32[32,8,128]{2,1,0:T(8,128)} %get-tuple-element.10), calls=%async_computation | async-start | bytes 262144 | tf_op jit(solution)/shard_map/all_to_all | solution.py:371
  18.6 0.2 fusion.20
  18.8 0.1 fusion.18
  18.9 0.0 copy-start
  18.9 0.7 %copy-done = f32[2,32]{1,0:T(2,128)S(1)} copy-done((f32[2,32]{1,0:T(2,128)S(1)}, f32[2,32]{1,0:T(2,128)}, u32[]{:S(2)}) %copy-start) | copy-done | bytes 280
  19.6 0.4 shard_map.73.matrix
  20.0 6.9 %all-to-all-done = f32[32,8,128]{2,1,0:T(8,128)S(1)} async-done(((f32[32,8,128]{2,1,0:T(8,128)}), f32[32,8,128]{2,1,0:T(8,128)S(1)}, u32[]{:S(2)}, u32[]{:S(2)}) %all-to-all-start) | async-done | bytes 131104 | tf_op jit(solution)/shard_map/all_to_all | solution.py:371
  26.9 0.9 %shard_map.77 = f32[512,128]{1,0:T(8,128)} custom-call(bf16[128,192]{1,0:T(8,128)(2,1)S(1)} %shard_map.73.matrix, f32[256,128]{1,0:T(8,128)S(1)} %bitcast.7), custom_call_target="tpu_custom_call" | custom-call | flops 16777216 | bytes 524288 | tf_op jit(solution)/shard_map/pallas_call | solution.py:272
  27.8 2.6 %all-to-all-start.1 = ((f32[32,16,128]{2,1,0:T(8,128)}), f32[32,16,128]{2,1,0:T(8,128)S(1)}, u32[]{:S(2)}, u32[]{:S(2)}) async-start(f32[32,16,128]{2,1,0:T(8,128)} %bitcast.5), calls=%async_computation.1 | async-start | bytes 524288 | tf_op jit(solution)/shard_map/all_to_all | solution.py:376
  30.4 1.4 %collective-permute-start.1 = (f32[24,128]{1,0:T(8,128)S(1)}, f32[24,128]{1,0:T(8,128)S(1)}, u32[]{:S(2)}, u32[]{:S(2)}) collective-permute-start(f32[24,128]{1,0:T(8,128)S(1)} %get-tuple-element.11), channel_id=1, source_target_pairs={{0,3},{1,4},{2,5},{3,6},{4,7},{5,8},{6,9},{7,10},{8,11},{9,12},{10... | collective-permute-start | bytes 36872 | tf_op jit(solution)/shard_map/ppermute | solution.py:362
  31.8 2.4 %collective-permute-start.2 = (f32[24,128]{1,0:T(8,128)S(1)}, f32[24,128]{1,0:T(8,128)S(1)}, u32[]{:S(2)}, u32[]{:S(2)}) collective-permute-start(f32[24,128]{1,0:T(8,128)S(1)} %get-tuple-element.12), channel_id=1, source_target_pairs={{0,11},{1,12},{2,13},{3,14},{4,15},{5,16},{6,17},{7,18},{8,19},{9,... | collective-permute-start | bytes 36872 | tf_op jit(solution)/shard_map/ppermute | solution.py:362
  34.3 2.0 %collective-permute-start.3 = (f32[24,128]{1,0:T(8,128)S(1)}, f32[24,128]{1,0:T(8,128)S(1)}, u32[]{:S(2)}, u32[]{:S(2)}) collective-permute-start(f32[24,128]{1,0:T(8,128)S(1)} %get-tuple-element.13), channel_id=1, source_target_pairs={{0,19},{1,20},{2,21},{3,22},{4,23},{5,24},{6,25},{7,26},{8,27},{9,... | collective-permute-start | bytes 36872 | tf_op jit(solution)/shard_map/ppermute | solution.py:362
  36.3 0.6 %collective-permute-start.5 = (f32[24,128]{1,0:T(8,128)S(1)}, f32[24,128]{1,0:T(8,128)S(1)}, u32[]{:S(2)}, u32[]{:S(2)}) collective-permute-start(f32[24,128]{1,0:T(8,128)S(1)} %get-tuple-element.11), channel_id=1, source_target_pairs={{0,2},{1,3},{2,4},{3,5},{4,6},{5,7},{6,8},{7,9},{8,10},{9,11},{10,... | collective-permute-start | bytes 36872 | tf_op jit(solution)/shard_map/ppermute | solution.py:362
  36.8 2.4 %collective-permute-start.6 = (f32[24,128]{1,0:T(8,128)S(1)}, f32[24,128]{1,0:T(8,128)S(1)}, u32[]{:S(2)}, u32[]{:S(2)}) collective-permute-start(f32[24,128]{1,0:T(8,128)S(1)} %get-tuple-element.12), channel_id=1, source_target_pairs={{0,10},{1,11},{2,12},{3,13},{4,14},{5,15},{6,16},{7,17},{8,18},{9,... | collective-permute-start | bytes 36872 | tf_op jit(solution)/shard_map/ppermute | solution.py:362
  39.3 0.8 %collective-permute-done.1.rest_0_ = f32[24,128]{1,0:T(8,128)S(1)} collective-permute-done((f32[24,128]{1,0:T(8,128)S(1)}, f32[24,128]{1,0:T(8,128)S(1)}, u32[]{:S(2)}, u32[]{:S(2)}) %collective-permute-start.1) | collective-permute-done | bytes 12320 | tf_op jit(solution)/shard_map/ppermute | solution.py:362
  40.0 2.8 %collective-permute-start.4 = (f32[24,128]{1,0:T(8,128)S(1)}, f32[24,128]{1,0:T(8,128)S(1)}, u32[]{:S(2)}, u32[]{:S(2)}) collective-permute-start(f32[24,128]{1,0:T(8,128)S(1)} %get-tuple-element.14), channel_id=1, source_target_pairs={{0,27},{1,28},{2,29},{3,30},{4,31},{5,0},{6,1},{7,2},{8,3},{9,4},{... | collective-permute-start | bytes 36872 | tf_op jit(solution)/shard_map/ppermute | solution.py:362
  42.8 0.0 collective-permute-done.2.rest_1_
  42.8 0.7 %collective-permute-start.7 = (f32[24,128]{1,0:T(8,128)S(1)}, f32[24,128]{1,0:T(8,128)S(1)}, u32[]{:S(2)}, u32[]{:S(2)}) collective-permute-start(f32[24,128]{1,0:T(8,128)S(1)} %get-tuple-element.13), channel_id=1, source_target_pairs={{0,18},{1,19},{2,20},{3,21},{4,22},{5,23},{6,24},{7,25},{8,26},{9,... | collective-permute-start | bytes 36872 | tf_op jit(solution)/shard_map/ppermute | solution.py:362
  43.5 0.0 collective-permute-done.3.rest_2_
  43.5 2.3 %collective-permute-start.8 = (f32[24,128]{1,0:T(8,128)S(1)}, f32[24,128]{1,0:T(8,128)S(1)}, u32[]{:S(2)}, u32[]{:S(2)}) collective-permute-start(f32[24,128]{1,0:T(8,128)S(1)} %get-tuple-element.14), channel_id=1, source_target_pairs={{0,26},{1,27},{2,28},{3,29},{4,30},{5,31},{6,0},{7,1},{8,2},{9,3},... | collective-permute-start | bytes 36872 | tf_op jit(solution)/shard_map/ppermute | solution.py:362
  45.8 0.0 collective-permute-done.4.rest_3_
  45.9 0.0 collective-permute-done.5.rest_4_
  45.9 0.0 collective-permute-done.6.rest_5_
  45.9 2.5 %collective-permute-done.7.rest_6_ = f32[24,128]{1,0:T(8,128)S(1)} collective-permute-done((f32[24,128]{1,0:T(8,128)S(1)}, f32[24,128]{1,0:T(8,128)S(1)}, u32[]{:S(2)}, u32[]{:S(2)}) %collective-permute-start.7) | collective-permute-done | bytes 12320 | tf_op jit(solution)/shard_map/ppermute | solution.py:362
  48.3 0.0 collective-permute-done.8.rest_7_
  48.3 0.0 all-to-all-done.1.fields
  48.3 5.8 %shard_map.78 = f32[2,128,128]{2,1,0:T(8,128)} custom-call(f32[32,16,128]{2,1,0:T(8,128)S(1)} %all-to-all-done.1.fields, f32[2,128,128]{2,1,0:T(8,128)S(1)} %copy-done.2, f32[24,128]{1,0:T(8,128)S(1)} %collective-permute-done.1.rest_0_, f32[24,128]{1,0:T(8,128)S(1)} %collective-permute-done.2.rest_1_, f32[24,128]{1,0:T(8,128)S(1)} %collective-permute-done.3.rest_2_, ...), custom_call_target="tpu_custom_call" | custom-call | flops 1543503872 | bytes 524288 | tf_op jit(solution)/shard_map/pallas_call | solution.py:272
  (3 shorter events, 0.0 us)
Async XLA Ops:
  0.0 8.9 %copy-start.1 = (f32[1,2,128,128]{3,2,1,0:T(8,128)S(1)}, f32[1,2,128,128]{3,2,1,0:T(8,128)}, u32[]{:S(2)}) copy-start(f32[1,2,128,128]{3,2,1,0:T(8,128)} %param.7) | copy-start | bytes 393220
  0.0 8.9 %copy-start.2 = (f32[2,128,128]{2,1,0:T(8,128)S(1)}, f32[2,128,128]{2,1,0:T(8,128)}, u32[]{:S(2)}) copy-start(f32[2,128,128]{2,1,0:T(8,128)} %propagator.5) | copy-start | bytes 393220
  2.3 6.6 %copy-start.3 = (f32[64,128]{1,0:T(8,128)S(1)}, f32[64,128]{1,0:T(8,128)}, u32[]{:S(2)}) copy-start(f32[64,128]{1,0:T(8,128)} %shard_map.74.state) | copy-start | bytes 98308
  2.3 8.3 %collective-permute-start = (f32[64,128]{1,0:T(8,128)}, f32[64,128]{1,0:T(8,128)S(1)}, u32[]{:S(2)}, u32[]{:S(2)}) collective-permute-start(f32[64,128]{1,0:T(8,128)} %shard_map.74.state), channel_id=1, source_target_pairs={{1,0},{2,1},{3,2},{4,3},{5,4},{6,5},{7,6},{8,7},{9,8},{10,9},{11,1... | collective-permute-start | bytes 98312 | tf_op jit(solution)/shard_map/ppermute | solution.py:350
  13.0 13.8 %all-to-all-start = ((f32[32,8,128]{2,1,0:T(8,128)}), f32[32,8,128]{2,1,0:T(8,128)S(1)}, u32[]{:S(2)}, u32[]{:S(2)}) async-start(f32[32,8,128]{2,1,0:T(8,128)} %get-tuple-element.10), calls=%async_computation | async-start | bytes 262144 | tf_op jit(solution)/shard_map/all_to_all | solution.py:371
  18.9 0.7 %copy-start = (f32[2,32]{1,0:T(2,128)S(1)}, f32[2,32]{1,0:T(2,128)}, u32[]{:S(2)}) copy-start(f32[2,32]{1,0:T(2,128)} %transmit.1) | copy-start | bytes 772
  27.8 20.5 %all-to-all-start.1 = ((f32[32,16,128]{2,1,0:T(8,128)}), f32[32,16,128]{2,1,0:T(8,128)S(1)}, u32[]{:S(2)}, u32[]{:S(2)}) async-start(f32[32,16,128]{2,1,0:T(8,128)} %bitcast.5), calls=%async_computation.1 | async-start | bytes 524288 | tf_op jit(solution)/shard_map/all_to_all | solution.py:376
  30.4 9.6 %collective-permute-start.1 = (f32[24,128]{1,0:T(8,128)S(1)}, f32[24,128]{1,0:T(8,128)S(1)}, u32[]{:S(2)}, u32[]{:S(2)}) collective-permute-start(f32[24,128]{1,0:T(8,128)S(1)} %get-tuple-element.11), channel_id=1, source_target_pairs={{0,3},{1,4},{2,5},{3,6},{4,7},{5,8},{6,9},{7,10},{8,11},{9,12},{10... | collective-permute-start | bytes 36872 | tf_op jit(solution)/shard_map/ppermute | solution.py:362
  31.8 11.0 %collective-permute-start.2 = (f32[24,128]{1,0:T(8,128)S(1)}, f32[24,128]{1,0:T(8,128)S(1)}, u32[]{:S(2)}, u32[]{:S(2)}) collective-permute-start(f32[24,128]{1,0:T(8,128)S(1)} %get-tuple-element.12), channel_id=1, source_target_pairs={{0,11},{1,12},{2,13},{3,14},{4,15},{5,16},{6,17},{7,18},{8,19},{9,... | collective-permute-start | bytes 36872 | tf_op jit(solution)/shard_map/ppermute | solution.py:362
  34.3 9.3 %collective-permute-start.3 = (f32[24,128]{1,0:T(8,128)S(1)}, f32[24,128]{1,0:T(8,128)S(1)}, u32[]{:S(2)}, u32[]{:S(2)}) collective-permute-start(f32[24,128]{1,0:T(8,128)S(1)} %get-tuple-element.13), channel_id=1, source_target_pairs={{0,19},{1,20},{2,21},{3,22},{4,23},{5,24},{6,25},{7,26},{8,27},{9,... | collective-permute-start | bytes 36872 | tf_op jit(solution)/shard_map/ppermute | solution.py:362
  36.3 9.6 %collective-permute-start.5 = (f32[24,128]{1,0:T(8,128)S(1)}, f32[24,128]{1,0:T(8,128)S(1)}, u32[]{:S(2)}, u32[]{:S(2)}) collective-permute-start(f32[24,128]{1,0:T(8,128)S(1)} %get-tuple-element.11), channel_id=1, source_target_pairs={{0,2},{1,3},{2,4},{3,5},{4,6},{5,7},{6,8},{7,9},{8,10},{9,11},{10,... | collective-permute-start | bytes 36872 | tf_op jit(solution)/shard_map/ppermute | solution.py:362
  36.8 9.0 %collective-permute-start.6 = (f32[24,128]{1,0:T(8,128)S(1)}, f32[24,128]{1,0:T(8,128)S(1)}, u32[]{:S(2)}, u32[]{:S(2)}) collective-permute-start(f32[24,128]{1,0:T(8,128)S(1)} %get-tuple-element.12), channel_id=1, source_target_pairs={{0,10},{1,11},{2,12},{3,13},{4,14},{5,15},{6,16},{7,17},{8,18},{9,... | collective-permute-start | bytes 36872 | tf_op jit(solution)/shard_map/ppermute | solution.py:362
  40.0 5.8 %collective-permute-start.4 = (f32[24,128]{1,0:T(8,128)S(1)}, f32[24,128]{1,0:T(8,128)S(1)}, u32[]{:S(2)}, u32[]{:S(2)}) collective-permute-start(f32[24,128]{1,0:T(8,128)S(1)} %get-tuple-element.14), channel_id=1, source_target_pairs={{0,27},{1,28},{2,29},{3,30},{4,31},{5,0},{6,1},{7,2},{8,3},{9,4},{... | collective-permute-start | bytes 36872 | tf_op jit(solution)/shard_map/ppermute | solution.py:362
  42.8 5.5 %collective-permute-start.7 = (f32[24,128]{1,0:T(8,128)S(1)}, f32[24,128]{1,0:T(8,128)S(1)}, u32[]{:S(2)}, u32[]{:S(2)}) collective-permute-start(f32[24,128]{1,0:T(8,128)S(1)} %get-tuple-element.13), channel_id=1, source_target_pairs={{0,18},{1,19},{2,20},{3,21},{4,22},{5,23},{6,24},{7,25},{8,26},{9,... | collective-permute-start | bytes 36872 | tf_op jit(solution)/shard_map/ppermute | solution.py:362
  43.5 4.8 %collective-permute-start.8 = (f32[24,128]{1,0:T(8,128)S(1)}, f32[24,128]{1,0:T(8,128)S(1)}, u32[]{:S(2)}, u32[]{:S(2)}) collective-permute-start(f32[24,128]{1,0:T(8,128)S(1)} %get-tuple-element.14), channel_id=1, source_target_pairs={{0,26},{1,27},{2,28},{3,29},{4,30},{5,31},{6,0},{7,1},{8,2},{9,3},... | collective-permute-start | bytes 36872 | tf_op jit(solution)/shard_map/ppermute | solution.py:362

commit v3 on v2

--- a/solution.py
+++ b/solution.py
@@ -15,6 +15,7 @@
 AXES = ("cuts", "group")
 F32 = jnp.float32
 BF16 = jnp.bfloat16
+KINDS = 4
 VMEM_LIMIT = 48 * 1024 * 1024
 WHOLE_VMEM = 60 * 1024 * 1024
 
@@ -120,27 +121,48 @@
 
 
 def kick_kernel(field_hbm, phases_hbm, energy_hbm, pixels_hbm, dest_hbm, out, field, phases, energy, pixels, dest, read_ref, sems):
-    blocks = phases.shape[0]
-    pairs = ((dest_hbm, dest), (field_hbm, field), (pixels_hbm, pixels), (phases_hbm, phases), (energy_hbm, energy))
+    blocks, size = phases.shape
+    pairs = ((field_hbm, field), (pixels_hbm, pixels), (phases_hbm, phases), (energy_hbm, energy), (dest_hbm, dest))
     copies = [pltpu.make_async_copy(source, target, sems.at[k]) for k, (source, target) in enumerate(pairs)]
     for copy in copies:
         copy.start()
     for copy in copies:
         copy.wait()
     new_phases, new_energy = kick(field[0], field[1], phases[...], energy[...], pixels[...], read_ref)
-    goals = [dest[0, block] for block in range(blocks)]
-    ranks = [0] * blocks
-    for later in range(blocks):
-        for earlier in range(later):
-            first = (goals[earlier] <= goals[later]).astype(jnp.int32)
-            ranks[later] = ranks[later] + first
-            ranks[earlier] = ranks[earlier] + (1 - first)
-    whole = pixels[...].astype(F32)
+    out[0:blocks, :] = new_phases
+    out[blocks : 2 * blocks, :] = new_energy
+    out[2 * blocks : 3 * blocks, :] = pixels[...].astype(F32)
+    square = (blocks, blocks)
+    own = lax.broadcasted_iota(jnp.int32, square, 0) == lax.broadcasted_iota(jnp.int32, square, 1)
+    goals = jnp.where(own, jnp.broadcast_to(dest[0:1, :].astype(F32), square), 0.0)
+    out[3 * blocks : 4 * blocks, :] = jnp.broadcast_to(jnp.sum(goals, axis=1, keepdims=True), (blocks, size))
+
+
+def by_destination(kinds):
+    goals = kinds[-1]
+    blocks = goals.shape[0]
+    place = lax.broadcasted_iota(jnp.int32, goals.shape, 0)
+    rank = jnp.zeros(goals.shape, jnp.int32)
     for block in range(blocks):
-        for kind, value in enumerate((new_phases, new_energy, whole)):
-            out[pl.ds(kind * blocks + ranks[block], 1), :] = value[block : block + 1, :]
-        goal = jnp.full((1, out.shape[1]), goals[block].astype(F32), F32)
-        out[pl.ds(3 * blocks + ranks[block], 1), :] = goal
+        goal = goals[block : block + 1]
+        ahead = (goal < goals) | ((goal == goals) & (place > block))
+        rank = rank + jnp.where(ahead, 1, 0)
+    ordered = [jnp.zeros(kind.shape, F32) for kind in kinds]
+    for block in range(blocks):
+        here = rank[block : block + 1] == place
+        ordered = [jnp.where(here, kind[block : block + 1], old) for kind, old in zip(kinds, ordered)]
+    return ordered
+
+
+def lane_groups(values, shifts):
+    size = values[0].shape[1]
+    group = lax.broadcasted_iota(jnp.int32, values[0].shape, 1) // (size // len(values))
+    joined_up = None
+    for k, (value, shift) in enumerate(zip(values, shifts)):
+        if shift % size:
+            value = pltpu.roll(value, shift % size, axis=1)
+        joined_up = value if joined_up is None else jnp.where(group == k, value, joined_up)
+    return joined_up
 
 
 def radiate_kernel(count, field, state, propagator, out, row_ref, spread_ref):
@@ -153,34 +175,43 @@
     out[1] = imag * keep
 
 
-def second_kernel(count, rows, cap, field, state, propagator, out, *rest):
+def second_kernel(count, rows, cap, height, field, state, propagator, out, *rest):
     sends = rest[:-3]
     read_ref, row_ref, spread_ref = rest[-3:]
-    blocks = state.shape[0] // 4
+    blocks, size = state.shape[0] // 4, state.shape[1]
     real, imag = field[0], field[1]
     grid = real.shape[0]
     pixels = state[2 * blocks : 3 * blocks, :].astype(jnp.int32)
     phases, energy = kick(real, imag, state[0:blocks, :], state[blocks : 2 * blocks, :], pixels, read_ref)
-    cuts = len(sends)
-    source = lax.rem(position() + 1, count)
-    cut = lax.div(source, count // cuts)
-    kinds = (phases, energy, state[2 * blocks : 3 * blocks, :])
-    for ahead, send in enumerate(sends):
-        wanted = lax.rem(cut + ahead, cuts).astype(F32)
-        chunk = [jnp.zeros((cap, phases.shape[1]), F32)] * 2 + [jnp.full((cap, phases.shape[1]), -1.0, F32)]
-        for start in range(0, blocks, cap):
-            goes = state[3 * blocks + start : 3 * blocks + start + cap, :] == wanted
-            chunk = [jnp.where(goes, kind[start : start + cap], old) for kind, old in zip(kinds, chunk)]
-        for kind in range(3):
-            send[kind * cap : (kind + 1) * cap, :] = chunk[kind]
+    kinds = by_destination((phases, energy, state[2 * blocks : 3 * blocks, :], state[3 * blocks : 4 * blocks, :]))
+    if height:
+        pieces = len(kinds)
+        width = size // pieces
+        for chunk in range(blocks // cap):
+            parts = [kind[chunk * cap : (chunk + 1) * cap] for kind in kinds]
+            for piece in range(pieces):
+                row = lane_groups(parts, [(k - piece) * width for k in range(pieces)])
+                out[pl.ds(piece * cap * height + 2 * rows + chunk, cap, stride=height), :] = row
+    else:
+        cuts = len(sends)
+        cut = lax.div(lax.rem(position() + 1, count), count // cuts)
+        for ahead, send in enumerate(sends):
+            wanted = lax.rem(cut + ahead, cuts).astype(F32)
+            chunk = [jnp.zeros((cap, size), F32)] * 2 + [jnp.full((cap, size), -1.0, F32)]
+            for start in range(0, blocks, cap):
+                goes = kinds[3][start : start + cap] == wanted
+                chunk = [jnp.where(goes, kind[start : start + cap], old) for kind, old in zip(kinds, chunk)]
+            for kind in range(3):
+                send[kind * cap : (kind + 1) * cap, :] = chunk[kind]
     real, imag = emit(real, imag, phases, pixels, row_ref, spread_ref)
     real, imag = diffract(real, imag, propagator)
     keep = kept_unless(count - 2)
     real, imag = real * keep, imag * keep
-    if rows:
+    if height:
         for part in range(grid // rows):
-            out[part, 0:rows, :] = real[part * rows : (part + 1) * rows]
-            out[part, rows : 2 * rows, :] = imag[part * rows : (part + 1) * rows]
+            base = part * height
+            out[base : base + rows, :] = real[part * rows : (part + 1) * rows]
+            out[base + rows : base + 2 * rows, :] = imag[part * rows : (part + 1) * rows]
     else:
         out[0] = real
         out[1] = imag
@@ -207,13 +238,16 @@
         out[base : base + 2 * count, :] = jnp.concatenate([high, high, low], axis=1)
 
 
-def filter_kernel(rows, matrix, data, out):
-    count = data.shape[0] // (2 * rows)
+def filter_kernel(rows, cuts, chunk_count, matrix, data, out):
+    count = matrix.shape[1] // 6
+    height = data.shape[0] // count
+    tall = out.shape[0] // count
+    groups = count // cuts
     size = data.shape[1]
     stacked = jnp.concatenate(
         [
             jnp.concatenate(
-                [data[pl.ds(part * rows + j, count, stride=2 * rows), :] for part in range(2)], axis=0
+                [data[pl.ds(part * rows + j, count, stride=height), :] for part in range(2)], axis=0
             )
             for j in range(rows)
         ],
@@ -223,9 +257,28 @@
     result = dot(matrix[...], jnp.concatenate([high, low, high], axis=0), 1, 0)
     for kind in range(4):
         for j in range(rows):
-            out[pl.ds(kind * rows + j, count, stride=4 * rows), :] = result[
+            out[pl.ds(kind * rows + j, count, stride=tall), :] = result[
                 kind * count : (kind + 1) * count, j * size : (j + 1) * size
             ]
+    bundles = [
+        pltpu.roll(data[pl.ds(2 * rows + chunk, count, stride=height), :], 1, axis=0)
+        for chunk in range(chunk_count)
+    ]
+    goals = [bundle[:, size - 1 : size] for bundle in bundles]
+    for cut in range(cuts):
+        chosen = bundles[0]
+        for bundle, goal in zip(bundles[1:], goals[1:]):
+            chosen = jnp.where(goal == float(cut), bundle, chosen)
+        for which in range(2):
+            first = cut * groups + 2 - which
+            fits = min(groups, count - first)
+            for source in range(cuts):
+                tile = chosen[source * groups : (source + 1) * groups]
+                base = 4 * rows + which * cuts + source
+                out[pl.ds(first * tall + base, fits, stride=tall), :] = tile[:fits]
+                for k in range(fits, groups):
+                    row = (first + k - count) * tall + base
+                    out[row : row + 1, :] = tile[k : k + 1]
 
 
 def joined(chunks_in):
@@ -237,21 +290,37 @@
     return kinds[0], kinds[1], kinds[2].astype(jnp.int32)
 
 
-def last_kernel(rows, fields, propagator, *rest):
+def relayed(fields, rows, cuts, which, count):
+    tall = fields.shape[0] // count
+    size = fields.shape[1]
+    width = size // KINDS
+    bundles = [
+        fields[pl.ds(4 * rows + which * cuts + cut, count, stride=tall), :] for cut in range(cuts)
+    ]
+    kinds = [lane_groups(bundles, [(cut - kind) * width for cut in range(cuts)]) for kind in range(KINDS)]
+    home = lax.rem(position() + (count - 2 + which), count)
+    wanted = lax.div(home, count // cuts).astype(F32)
+    return kinds[0], kinds[1], jnp.where(kinds[3] == wanted, kinds[2], -1.0).astype(jnp.int32)
+
+
+def last_kernel(rows, cuts, count, fields, propagator, *rest):
     out, field_ref, read_ref, row_ref, spread_ref = rest[-5:]
-    half = (len(rest) - 5) // 2
-    first_phases, first_energy, first_pixels = joined(rest[:half])
-    phases, energy, next_pixels = joined(rest[half : 2 * half])
+    chunks_in = rest[:-5]
     grid = propagator.shape[1]
-    if rows:
+    if chunks_in:
+        half = len(chunks_in) // 2
+        first_phases, first_energy, first_pixels = joined(chunks_in[:half])
+        phases, energy, next_pixels = joined(chunks_in[half:])
+        for kind in range(4):
+            field_ref[kind] = fields[kind]
+    else:
+        first_phases, first_energy, first_pixels = relayed(fields, rows, cuts, 0, count)
+        phases, energy, next_pixels = relayed(fields, rows, cuts, 1, count)
+        tall = fields.shape[0] // count
         for part in range(grid // rows):
             for kind in range(4):
-                field_ref[kind, part * rows : (part + 1) * rows, :] = fields[
-                    part, kind * rows : (kind + 1) * rows, :
-                ]
-    else:
-        for kind in range(4):
-            field_ref[kind] = fields[kind]
+                base = part * tall + kind * rows
+                field_ref[kind, part * rows : (part + 1) * rows, :] = fields[base : base + rows, :]
     real, imag = field_ref[0], field_ref[1]
     first_phases, _ = kick(real, imag, first_phases, first_energy, first_pixels, read_ref.at[0])
     real, imag = emit(real, imag, first_phases, first_pixels, row_ref, spread_ref)
@@ -326,6 +395,10 @@
     blocks, size = phases.shape[1:]
     cap = max(2, 2 * blocks // cuts)
     rows = grid // count if grid % count == 0 and (2 * grid // count) % 8 == 0 else 0
+    if cap * KINDS != count or cuts != KINDS or size % 128 or blocks != 2 * cap or groups % 8:
+        rows = 0
+    height = 2 * rows + 8 if rows else 0
+    tall = 4 * rows + 8
     field = radiation[0]
     shape = lambda *dims: jax.ShapeDtypeStruct(dims, F32)
     read = lambda number: pltpu.VMEM((2, number, size), F32)
@@ -340,7 +413,7 @@
             pltpu.VMEM((blocks, size), F32),
             pltpu.VMEM((blocks, size), F32),
             pltpu.VMEM((blocks, size), jnp.int32),
-            pltpu.SMEM((1, blocks), jnp.int32),
+            pltpu.VMEM((1, blocks), jnp.int32),
             read(blocks),
             pltpu.SemaphoreType.DMA((5,)),
         ],
@@ -352,9 +425,10 @@
         functools.partial(radiate_kernel, count), shape(2, grid, grid), hot(blocks), pass_flops + prop_flops,
         (field, state, propagator),
     )
-    part_shape = shape(count, 2 * rows, grid) if rows else shape(2, grid, grid)
+    part_shape = shape(count * height, grid) if rows else shape(2, grid, grid)
+    send_shapes = [] if rows else [shape(3 * cap, size)] * cuts
     field, *sends = call(
-        functools.partial(second_kernel, count, rows, cap), (part_shape, *[shape(3 * cap, size)] * cuts),
+        functools.partial(second_kernel, count, rows, cap, height), (part_shape, *send_shapes),
         [read(blocks)] + hot(blocks), 2 * pass_flops + prop_flops,
         (field, behind, propagator),
     )
@@ -368,19 +442,22 @@
             matrix_kernel, jax.ShapeDtypeStruct((4 * count, 6 * count), BF16), [], 1 << 20,
             (transmit, *time_tables(count)),
         )
-        data = lax.all_to_all(field, AXES, split_axis=0, concat_axis=0, tiled=True)
+        data = lax.all_to_all(
+            field.reshape(count, height, grid), AXES, split_axis=0, concat_axis=0, tiled=True
+        )
         sent = call(
-            functools.partial(filter_kernel, rows), shape(count * 4 * rows, grid), [], 1 << 24,
-            (matrix, data.reshape(count * 2 * rows, grid)),
+            functools.partial(filter_kernel, rows, cuts, blocks // cap), shape(count * tall, grid), [], 1 << 24,
+            (matrix, data.reshape(count * height, grid)),
         )
         fields = lax.all_to_all(
-            sent.reshape(count, 4 * rows, grid), AXES, split_axis=0, concat_axis=0, tiled=True
+            sent.reshape(count, tall, grid), AXES, split_axis=0, concat_axis=0, tiled=True
         )
+        fields = fields.reshape(count * tall, grid)
     else:
         fields = filter_any(field, transmit, count)
     capacity = cuts * cap
     out = call(
-        functools.partial(last_kernel, rows), shape(2, grid, grid),
+        functools.partial(last_kernel, rows, cuts, count), shape(2, grid, grid),
         [pltpu.VMEM((4, grid, grid), F32), pltpu.VMEM((2, 2, capacity, size), F32)] + hot(capacity),
         10 * pass_flops + 2 * prop_flops, (fields, propagator, *chunks_in),
     )

time: 54.4 us -> 51 us (0.938)
  starting transfers between devices: 29.3 us -> 12 us
  blocking collectives: 0 us -> 15.4 us
  waiting for transfers between devices: 10.7 us -> 9.85 us
  Pallas kernels: 12.9 us -> 12.3 us
    all_to_all x0 -> x1, blocking collectives: none -> 15.4 us  [on_device(): lax.all_to_all(sent.reshape(count, tall, grid), AXES, split_axis=0, conca...]
    ppermute x8 -> x0, starting transfers between devices: 14.7 us -> none  [on_device(): lax.ppermute(send, AXES, [(i, (i + lag + groups * ahead) % count) for i i...]
    ppermute x8 -> x0, waiting for transfers between devices: 3.23 us -> none  [on_device(): lax.ppermute(send, AXES, [(i, (i + lag + groups * ahead) % count) for i i...]
    all_to_all x2 -> x1, starting transfers between devices: 8.18 us -> 5.6 us  [on_device(): lax.all_to_all(field.reshape(count, height, grid), AXES, split_axis=0, co...]
    all_to_all x2 -> x1, waiting for transfers between devices: 6.86 us -> 9.21 us  [on_device(): lax.all_to_all(field.reshape(count, height, grid), AXES, split_axis=0, co...]
    pallas_call x6, Pallas kernels: 12.9 us -> 12.3 us  [call(): pl.pallas_call(kernel, out_shape=out_shape, in_specs=specs, out_specs=jax...]
  transfers between devices with their start and end apart: 11 -> 2, of which waited for: 4 -> 2; matrix products, arithmetic and copies ran while one was open for 1% -> 1% of each run, Pallas kernels for 3% -> 3%
where the time goes in v3:
time: 51 us; the launch traced here: 50.8 us
  blocking collectives  15.4 us (30%)
  Pallas kernels  12.3 us (24%)
  starting transfers between devices  12 us (24%)
  waiting for transfers between devices  9.85 us (19%)
  local copies, waits for them, and re-layouts  0.69 us (1%)
    all_to_all x1, blocking collectives, on_device(): lax.all_to_all(sent.reshape(count, tall, grid), AXES, split_axis=0, conca...  15.4 us
    pallas_call x6, Pallas kernels, call(): pl.pallas_call(kernel, out_shape=out_shape, in_specs=specs, out_specs=jax...  12.3 us
    all_to_all x1, waiting for transfers between devices, on_device(): lax.all_to_all(field.reshape(count, height, grid), AXES, split_axis=0, co...  9.21 us
    ppermute x1, starting transfers between devices, on_device(): behind = lax.ppermute(state, AXES, route)  6.43 us
    all_to_all x1, starting transfers between devices, on_device(): lax.all_to_all(field.reshape(count, height, grid), AXES, split_axis=0, co...  5.6 us
  transfers between devices with their start and end apart: 2, of which 2 were waited for; matrix products, arithmetic and copies ran while one was open for 1% of the time, Pallas kernels for 3%

profile of v3, /device:TPU:0, one launch (start us, length us, event | category | flops | bytes accessed | tf_op | source)
XLA Modules:
  0.0 50.8 jit_solution(4271252604185917801)
XLA Ops:
  0.0 0.0 copy-start.1
  0.0 0.0 copy-start.2
  0.0 2.2 %shard_map.74.state = f32[64,128]{1,0:T(8,128)} custom-call(f32[2,128,128]{2,1,0:T(8,128)} %bitcast.12, f32[16,128]{1,0:T(8,128)} %bitcast.14, f32[16,128]{1,0:T(8,128)} %bitcast.15, s32[16,128]{1,0:T(8,128)} %bitcast.16, s32[1,16]{1,0:T(1,128)} %dest_hbm.1), custom_call_target="tpu_custom_call" | custom-call | flops 134217728 | bytes 524288 | tf_op jit(solution)/shard_map/pallas_call | solution.py:341
  2.2 0.0 copy-start.3
  2.3 6.4 %collective-permute-start = (f32[64,128]{1,0:T(8,128)}, f32[64,128]{1,0:T(8,128)S(1)}, u32[]{:S(2)}, u32[]{:S(2)}) collective-permute-start(f32[64,128]{1,0:T(8,128)} %shard_map.74.state), channel_id=1, source_target_pairs={{1,0},{2,1},{3,2},{4,3},{5,4},{6,5},{7,6},{8,7},{9,8},{10,9},{11,1... | collective-permute-start | bytes 98312 | tf_op jit(solution)/shard_map/ppermute | solution.py:423
  8.7 0.2 fusion.20
  8.8 0.0 copy-done.1
  8.9 0.0 copy-done.2
  8.9 0.0 copy-done.3
  8.9 1.1 %shard_map.75.field = f32[2,128,128]{2,1,0:T(8,128)S(1)} custom-call(f32[2,128,128]{2,1,0:T(8,128)S(1)} %bitcast.13, f32[64,128]{1,0:T(8,128)S(1)} %copy-done.3, f32[2,128,128]{2,1,0:T(8,128)S(1)} %copy-done.2), custom_call_target="tpu_custom_call" | custom-call | flops 234881024 | bytes 524288 | tf_op jit(solution)/shard_map/pallas_call | solution.py:341
  10.0 0.6 %collective-permute-done.state = f32[64,128]{1,0:T(8,128)S(1)} collective-permute-done((f32[64,128]{1,0:T(8,128)}, f32[64,128]{1,0:T(8,128)S(1)}, u32[]{:S(2)}, u32[]{:S(2)}) %collective-permute-start) | collective-permute-done | bytes 32800 | tf_op jit(solution)/shard_map/ppermute | solution.py:423
  10.6 2.5 %shard_map.76 = f32[512,128]{1,0:T(8,128)} custom-call(f32[2,128,128]{2,1,0:T(8,128)S(1)} %shard_map.75.field, f32[64,128]{1,0:T(8,128)S(1)} %collective-permute-done.state, f32[2,128,128]{2,1,0:T(8,128)S(1)} %copy-done.2), custom_call_target="tpu_custom_call" | custom-call | flops 369098752 | bytes 524288 | tf_op jit(solution)/shard_map/pallas_call | solution.py:341
  13.1 5.6 %all-to-all-start = ((f32[32,16,128]{2,1,0:T(8,128)}), f32[32,16,128]{2,1,0:T(8,128)S(1)}, u32[]{:S(2)}, u32[]{:S(2)}) async-start(f32[32,16,128]{2,1,0:T(8,128)} %bitcast.4), calls=%async_computation | async-start | bytes 524288 | tf_op jit(solution)/shard_map/all_to_all | solution.py:445
  18.7 0.1 fusion.18
  18.8 0.2 fusion.22
  19.0 0.0 copy-start
  19.0 0.7 %copy-done = f32[2,32]{1,0:T(2,128)S(1)} copy-done((f32[2,32]{1,0:T(2,128)S(1)}, f32[2,32]{1,0:T(2,128)}, u32[]{:S(2)}) %copy-start) | copy-done | bytes 280
  19.7 0.4 shard_map.73.matrix
  20.1 9.2 %all-to-all-done = f32[32,16,128]{2,1,0:T(8,128)S(1)} async-done(((f32[32,16,128]{2,1,0:T(8,128)}), f32[32,16,128]{2,1,0:T(8,128)S(1)}, u32[]{:S(2)}, u32[]{:S(2)}) %all-to-all-start) | async-done | bytes 262176 | tf_op jit(solution)/shard_map/all_to_all | solution.py:445
  29.3 0.2 shard_map.77
  29.6 15.4 %all_to_all.10 = f32[32,24,128]{2,1,0:T(8,128)S(1)} all-to-all(f32[32,24,128]{2,1,0:T(8,128)S(1)} %bitcast.9), channel_id=1, replica_groups=mesh['cuts'=4,'group'=8] {'cuts','group'}, dimensions={0} | all-to-all | bytes 786432 | tf_op jit(solution)/shard_map/all_to_all | solution.py:452
  44.9 5.8 %shard_map.78 = f32[2,128,128]{2,1,0:T(8,128)} custom-call(f32[768,128]{1,0:T(8,128)S(1)} %bitcast.11, f32[2,128,128]{2,1,0:T(8,128)S(1)} %copy-done.2), custom_call_target="tpu_custom_call" | custom-call | flops 1543503872 | bytes 524288 | tf_op jit(solution)/shard_map/pallas_call | solution.py:341
  (3 shorter events, 0.0 us)
Async XLA Ops:
  0.0 8.8 %copy-start.1 = (f32[1,2,128,128]{3,2,1,0:T(8,128)S(1)}, f32[1,2,128,128]{3,2,1,0:T(8,128)}, u32[]{:S(2)}) copy-start(f32[1,2,128,128]{3,2,1,0:T(8,128)} %param.7) | copy-start | bytes 393220
  0.0 8.9 %copy-start.2 = (f32[2,128,128]{2,1,0:T(8,128)S(1)}, f32[2,128,128]{2,1,0:T(8,128)}, u32[]{:S(2)}) copy-start(f32[2,128,128]{2,1,0:T(8,128)} %propagator.5) | copy-start | bytes 393220
  2.2 6.6 %copy-start.3 = (f32[64,128]{1,0:T(8,128)S(1)}, f32[64,128]{1,0:T(8,128)}, u32[]{:S(2)}) copy-start(f32[64,128]{1,0:T(8,128)} %shard_map.74.state) | copy-start | bytes 98308
  2.3 8.3 %collective-permute-start = (f32[64,128]{1,0:T(8,128)}, f32[64,128]{1,0:T(8,128)S(1)}, u32[]{:S(2)}, u32[]{:S(2)}) collective-permute-start(f32[64,128]{1,0:T(8,128)} %shard_map.74.state), channel_id=1, source_target_pairs={{1,0},{2,1},{3,2},{4,3},{5,4},{6,5},{7,6},{8,7},{9,8},{10,9},{11,1... | collective-permute-start | bytes 98312 | tf_op jit(solution)/shard_map/ppermute | solution.py:423
  13.1 16.2 %all-to-all-start = ((f32[32,16,128]{2,1,0:T(8,128)}), f32[32,16,128]{2,1,0:T(8,128)S(1)}, u32[]{:S(2)}, u32[]{:S(2)}) async-start(f32[32,16,128]{2,1,0:T(8,128)} %bitcast.4), calls=%async_computation | async-start | bytes 524288 | tf_op jit(solution)/shard_map/all_to_all | solution.py:445
  19.0 0.7 %copy-start = (f32[2,32]{1,0:T(2,128)S(1)}, f32[2,32]{1,0:T(2,128)}, u32[]{:S(2)}) copy-start(f32[2,32]{1,0:T(2,128)} %transmit.1) | copy-start | bytes 772
